TPU v7x, 128 devices: a whole 4x4x4 slice. The times are simulated.
128 devices in a mesh: dp: 2 (over z_lo), cfg: 2 (over core), pipe: 8 (over z_hi, x), seq: 4 (over y).
Axes of the slice: x: 4, y: 4, z: 4 (z_hi: 2, z_lo: 2; z = z_hi * 2 + z_lo), core: 2. Of those that a mesh axis runs over, the one named last changes fastest.
Arguments:
- image_states: bfloat16 [2, 8192, 3072], P('cfg', ('dp', 'pipe', 'seq')), parts along dimension 1, may hold values from -600 to 600
- prompt_states: bfloat16 [2, 512, 3072], P('cfg', ('dp', 'seq')), parts along dimension 1, may hold values from -6 to 6
- stale_kv: bfloat16 [2, 2, 8192, 1536], P('cfg', None, ('dp', 'pipe', 'seq')), parts along dimension 2, may hold values from -140 to 140
- w_image_qkv: bfloat16 [3, 3072, 1536], P(None, None, 'seq'), may hold values from -0.109375 to 0.109375
- w_prompt_kv: bfloat16 [2, 3072, 1536], P(None, None, 'seq'), may hold values from -0.109375 to 0.109375
- w_output: bfloat16 [1536, 3072], P('seq'), may hold values from -0.5 to 0.5
- mod_table: float32 [50, 3, 3072], replicated, may hold values from -4 to 4
- timestep: int32 [2], P('dp'), parts along dimension 0, may hold values from 0 to 49
- guidance: float32 [2], P('dp'), parts along dimension 0, may hold values from 4 to 8
Outputs:
- guided: bfloat16 [8192, 3072], P(('dp', 'pipe', 'seq'), 'cfg'), parts along dimension 0
There are 2 independent parts, one for each index of `dp`. A program takes and returns all parts, laid end to end along the dimension named above; an argument that names none is the same for every part. Nothing has to cross between parts.
All inputs are finite; a program needn't handle non-finite values.
Results may differ from a plain program's by a relative error of at most 0.015.
The roundings to bfloat16 on the way count: a program that leaves them out, or rounds other values in their place, can miss the bound.
Values may be sent and summed in bfloat16 or wider, within the bound.
A program may use at most 128 MiB of HBM per device.

v0:
```python
import math

import jax
import jax.numpy as jnp
from jax import lax
from jax.sharding import PartitionSpec as P

HEAD_DIM = 128


def from_partner(block, axis, distance):
    count = lax.axis_size(axis)
    route = []
    for low in range(count):
        high = low | 1 << distance
        if high != low and high < count:
            route += [(low, high), (high, low)]
    return lax.ppermute(block, axis, route)


def layer_norm(values):
    center = values - jnp.mean(values, axis=-1, keepdims=True)
    spread = jnp.mean(center * center, axis=-1, keepdims=True)
    return center * lax.rsqrt(spread + 1e-06)


def local(
    image_states,
    prompt_states,
    stale_kv,
    w_image_qkv,
    w_prompt_kv,
    w_output,
    mod_table,
    timestep,
    guidance,
):
    mod_rows = lax.dynamic_index_in_dim(mod_table, timestep[0], 0, keepdims=False)
    modulated = (
        layer_norm(image_states[0].astype(jnp.float32)) * (1.0 + mod_rows[1]) + mod_rows[0]
    ).astype(jnp.bfloat16)
    projections = jnp.einsum(
        "td,cde->cte",
        lax.all_gather(modulated, "seq", axis=0, tiled=True),
        w_image_qkv,
        preferred_element_type=jnp.float32,
    ).astype(jnp.bfloat16)
    prompt_norm = layer_norm(prompt_states[0].astype(jnp.float32)).astype(jnp.bfloat16)
    prompt_pair = jnp.einsum(
        "td,cde->cte",
        lax.all_gather(prompt_norm, "seq", axis=0, tiled=True),
        w_prompt_kv,
        preferred_element_type=jnp.float32,
    ).astype(jnp.bfloat16)
    patch_len = projections.shape[1]
    local_width = projections.shape[2]
    heads_here = local_width // HEAD_DIM
    queries = projections[0].reshape(patch_len, heads_here, HEAD_DIM)
    fresh_pair = projections[1:3]
    section_id = lax.axis_index("pipe")
    factor = 1.0 / math.sqrt(HEAD_DIM)

    def absorb(running, key_rows, value_rows, keep_mask):
        maxima, totals, accumulated = running
        row_count = key_rows.shape[0]
        key_rows = key_rows.reshape(row_count, heads_here, HEAD_DIM)
        value_rows = value_rows.reshape(row_count, heads_here, HEAD_DIM)
        scores = (
            jnp.einsum("qhd,khd->hqk", queries, key_rows, preferred_element_type=jnp.float32)
            * factor
        )
        scores = jnp.where(keep_mask[None, None, :], scores, -1e30)
        new_maxima = jnp.maximum(maxima, jnp.max(scores, axis=-1))
        correction = jnp.exp(maxima - new_maxima)
        weights = jnp.exp(scores - new_maxima[..., None])
        totals = totals * correction + jnp.sum(weights, axis=-1)
        accumulated = accumulated * correction[..., None] + jnp.einsum(
            "hqk,khd->hqd",
            weights.astype(jnp.bfloat16),
            value_rows,
            preferred_element_type=jnp.float32,
        )
        return (new_maxima, totals, accumulated)

    start_state = (
        jnp.full((heads_here, patch_len), -1e30, jnp.float32),
        jnp.zeros((heads_here, patch_len), jnp.float32),
        jnp.zeros((heads_here, patch_len, HEAD_DIM), jnp.float32),
    )
    own_keys = jnp.concatenate([prompt_pair[0], fresh_pair[0]], axis=0)
    own_values = jnp.concatenate([prompt_pair[1], fresh_pair[1]], axis=0)
    running = absorb(start_state, own_keys, own_values, jnp.ones((own_keys.shape[0],), jnp.bool_))
    stale_heads = lax.all_to_all(stale_kv[0], "seq", split_axis=2, concat_axis=1, tiled=True)
    shard_piece = lax.all_gather(fresh_pair, "pipe", axis=1, tiled=True)
    row_count = shard_piece.shape[1]
    keep_mask = jnp.arange(row_count, dtype=jnp.int32) // patch_len < section_id
    needed = jnp.int32(0) // patch_len < section_id

    def taken(state):
        return absorb(state, shard_piece[0], shard_piece[1], keep_mask)

    def skipped(state):
        return state

    running = lax.cond(needed, taken, skipped, running)
    add_shard_piece = lax.all_gather(stale_heads, "pipe", axis=1, tiled=True)
    row_count = add_shard_piece.shape[1]
    add_keep_mask = jnp.arange(row_count, dtype=jnp.int32) // patch_len > section_id
    needed = (jnp.int32(0) + row_count - 1) // patch_len > section_id

    def taken(state):
        return absorb(state, add_shard_piece[0], add_shard_piece[1], add_keep_mask)

    def skipped(state):
        return state

    running = lax.cond(needed, taken, skipped, running)
    maxima, totals, accumulated = running
    attended = jnp.transpose(accumulated / totals[..., None], (1, 0, 2)).reshape(
        patch_len, local_width
    )
    partner = from_partner(attended, "cfg", 0)
    cfg_side = lax.axis_index("cfg")
    is_cond = cfg_side == 0
    cond_part = jnp.where(is_cond, attended, partner)
    uncond = jnp.where(is_cond, partner, attended)
    mixed = (uncond + guidance[0] * (cond_part - uncond)).astype(jnp.bfloat16)
    half_width = w_output.shape[1] // 2
    w_half = lax.dynamic_slice_in_dim(w_output, cfg_side * half_width, half_width, 1)
    summed = lax.psum_scatter(
        jnp.dot(mixed, w_half, preferred_element_type=jnp.float32),
        "seq",
        scatter_dimension=0,
        tiled=True,
    )
    gate_half = lax.dynamic_slice_in_dim(mod_rows[2], cfg_side * half_width, half_width, 0)
    return (gate_half * summed).astype(jnp.bfloat16)


def solution(mesh):
    return jax.shard_map(
        local,
        mesh=mesh,
        in_specs=(
            P("cfg", ("dp", "pipe", "seq"), None),
            P("cfg", ("dp", "seq"), None),
            P("cfg", None, ("dp", "pipe", "seq"), None),
            P(None, None, "seq"),
            P(None, None, "seq"),
            P("seq", None),
            P(),
            P("dp"),
            P("dp"),
        ),
        out_specs=P(("dp", "pipe", "seq"), "cfg"),
        check_vma=False,
    )
```

profile of v0, /device:TPU:6, one launch (start us, length us, event | category | flops | bytes accessed | tf_op | source)
XLA Modules:
  0.0 387.0 jit_solution(8808631681631446233)
XLA Ops:
  7.4 1.4 convert_reduce_fusion
  8.7 1.5 fusion.33
  10.2 1.0 dynamic-slice_add_fusion
  11.2 2.4 fusion.36
  13.7 1.1 convert_reduce_fusion.1
  14.9 1.3 fusion.59
  16.1 0.9 fusion.60
  17.1 38.5 %all-gather.5.cloned.1.call-done = bf16[512,3072]{1,0:T(8,128)(2,1)} async-done(((bf16[128,3072]{1,0:T(8,128)(2,1)}), bf16[512,3072]{1,0:T(8,128)(2,1)}) %all-gather.5.cloned.1.call-update) | async-done | bytes 3145744 | tf_op jit(solution)/shard_map/all_gather | solution.py:44
  55.7 7.8 %fusion.42 = bf16[3,512,384]{1,2,0:T(8,128)(2,1)S(1)} fusion(bf16[3,3072,384]{2,1,0:T(8,128)(2,1)} %param.16, bf16[512,3072]{1,0:T(8,128)(2,1)} %all-gather.5.cloned.1.call-done), kind=kOutput, calls=%fused_computation.47 | convolution fusion | flops 3624468480 | bytes 11403264 | tf_op jit(solution)/shard_map/td,cde->cte/dot_general | solution.py:42
  63.5 1.0 copy-done.2
  64.5 1.0 slice.58
  65.6 2.3 copy.49
  67.9 24.4 %all_to_all.18 = bf16[2,128,1536]{1,0,2:T(2,128)(2,1)S(1)} all-to-all(bf16[2,128,1536]{1,0,2:T(2,128)(2,1)S(1)} %bitcast.89), channel_id=1, replica_groups=mesh['dp'=2,'cfg'=2,'pipe'=8,'seq'=4] {'seq'}, dimensions={2} | all-to-all | bytes 1572864 | tf_op jit(solution)/shard_map/all_to_all | solution.py:93
  92.3 0.6 copy.50
  92.9 1.2 all_to_all.16
  94.2 0.6 add_select_fusion
  94.8 4.2 %fusion.51 = bf16[2,256,384]{2,1,0:T(8,128)(2,1)S(1)} fusion(bf16[2,3072,384]{2,1,0:T(8,128)(2,1)} %param.17, bf16[256,3072]{1,0:T(8,128)(2,1)} %all-gather.7.cloned.1.call-done), kind=kOutput, calls=%fused_computation.50 | convolution fusion | flops 1208156160 | bytes 6684672 | tf_op jit(solution)/shard_map/td,cde->cte/dot_general | solution.py:49
  99.0 0.1 copy.41
  99.2 0.8 copy.42
  100.2 0.8 copy.46
  101.0 2.1 fusion.80
  103.1 1.2 copy.43
  104.3 0.9 copy.47
  105.2 1.9 multiply_reduce_fusion
  107.2 1.0 fusion.23
  108.2 1.5 fusion.45
  109.8 84.0 %all-gather.9.cloned.1.call-done = bf16[2,4096,384]{1,2,0:T(8,128)(2,1)} async-done(((bf16[2,512,384]{1,2,0:T(8,128)(2,1)}), bf16[2,4096,384]{1,2,0:T(8,128)(2,1)}) %all-gather.9.cloned.1.call-update) | async-done | bytes 6291472 | tf_op jit(solution)/shard_map/all_gather | solution.py:94
  193.8 37.4 %conditional.2 = ((f32[3,512]{1,0:T(4,128)S(1)}, f32[3,512]{1,0:T(4,128)S(1)}, f32[3,512,128]{2,1,0:T(8,128)S(1)})) conditional(s32[]{:T(128)} %convert_element_type.52, (f32[3,512]{1,0:T(4,128)S(1)}, f32[3,512]{1,0:T(4,128)S(1)}, f32[3,512,128]{2,1,0:T(8,128)S(1)}) %tuple.19, (s32[]{:T(128)}, s32[4096]{0:T(1024)}, bf16[2,4096,384]{1,2,0:T(8,128)(2,1)}, ...), branch_computations={%region_6.7_spmd, %region_7.10_spmd} | conditional | flops 3290831872 | bytes 96469024 | solution.py:105
  193.8 0.7 broadcast_compare_fusion
  194.5 3.5 fusion.78
  198.0 11.1 %fusion = (f32[3,512]{1,0:T(4,128)S(1)}, f32[3,512,4096]{2,1,0:T(8,128)}) fusion(pred[4096]{0:T(1024)(128)(4,1)S(1)} %broadcast_compare_fusion, bf16[512,3,128]{0,2,1:T(8,128)(2,1)S(1)} %get-tuple-element.102, bf16[4096,3,128]{0,2,1:T(8,128)(2,1)S(1)} %bitcast.81), kind=kOutput, calls=%fused_computation.2 | convolution fusion | flops 1629485568 | bytes 28715008 | tf_op jit(solution)/shard_map/cond/branch_1_fun/qhd,khd->hqk/dot_general | solution.py:69
  209.1 11.3 %fusion.2 = f32[3,512]{1,0:T(4,128)S(1)} fusion(f32[3,512,4096]{2,1,0:T(8,128)} %get-tuple-element.123, f32[3,512]{1,0:T(4,128)S(1)} %max.4, pred[4096]{0:T(1024)(128)(4,1)S(1)} %broadcast_compare_fusion), kind=kLoop, calls=%fused_computation.4 | loop fusion | flops 25164288 | bytes 25182208 | tf_op jit(solution)/shard_map/cond/branch_1_fun/reduce_sum | solution.py:76
  220.4 10.8 %fusion.6 = f32[3,512,128]{2,1,0:T(8,128)S(1)} fusion(bf16[4096,3,128]{0,2,1:T(8,128)(2,1)S(1)} %bitcast.90, f32[3,512,4096]{2,1,0:T(8,128)} %get-tuple-element.123, f32[3,512]{1,0:T(4,128)S(1)} %max.4, pred[4096]{0:T(1024)(128)(4,1)S(1)} %broadcast_compare_fusion, f32[3,512,128]{2,1,0:T(8,128)S(1)} %get-tuple-element.53, f32[3,512]{1,0:T(4,128)S(1)} %get-tuple-element.117), kind=kOutput, calls=%fused_computation.7 | convolution fusion | flops 1636171776 | bytes 29900800 | tf_op jit(solution)/shard_map/cond/branch_1_fun/hqk,khd->hqd/dot_general | solution.py:77
  231.2 62.8 %all-gather.11.cloned.1.call-done = bf16[2,4096,384]{1,2,0:T(8,128)(2,1)} async-done(((bf16[2,512,384]{1,2,0:T(8,128)(2,1)}), bf16[2,4096,384]{1,2,0:T(8,128)(2,1)}) %all-gather.11.cloned.1.call-update) | async-done | bytes 6291472 | tf_op jit(solution)/shard_map/all_gather | solution.py:106
  293.9 39.3 %conditional.3 = (f32[3,512]{1,0:T(4,128)S(1)}, f32[3,512,128]{1,2,0:T(8,128)S(1)}) conditional(s32[]{:T(128)} %convert_element_type.51, (f32[3,512]{1,0:T(4,128)S(1)}, f32[3,512,128]{2,1,0:T(8,128)S(1)}) %tuple.21, (s32[]{:T(128)}, s32[4096]{0:T(1024)}, bf16[2,4096,384]{1,2,0:T(8,128)(2,1)}, bf16[512,3,128]{0,2,1:T(8,128)(2,1)S(1)}, ...), branch_computations={%region_10.11_spmd, %region_11.14_spmd} | conditional | flops 3290831872 | bytes 98029584 | solution.py:117
  293.9 0.7 broadcast_compare_fusion.1
  294.6 3.5 fusion.79
  298.1 10.5 %fusion.11 = (f32[3,512]{1,0:T(4,128)S(1)}, f32[3,512,4096]{2,1,0:T(8,128)}) fusion(pred[4096]{0:T(1024)(128)(4,1)S(1)} %broadcast_compare_fusion.1, bf16[512,3,128]{0,2,1:T(8,128)(2,1)S(1)} %get-tuple-element.109, bf16[4096,3,128]{0,2,1:T(8,128)(2,1)S(1)} %bitcast.82), kind=kOutput, calls=%fused_computation.15 | convolution fusion | flops 1629485568 | bytes 28715008 | tf_op jit(solution)/shard_map/cond/branch_1_fun/qhd,khd->hqk/dot_general | solution.py:69
  308.7 11.3 %fusion.13 = f32[3,512]{1,0:T(4,128)S(1)} fusion(f32[3,512,4096]{2,1,0:T(8,128)} %get-tuple-element.127, f32[3,512]{1,0:T(4,128)S(1)} %max.5, pred[4096]{0:T(1024)(128)(4,1)S(1)} %broadcast_compare_fusion.1), kind=kLoop, calls=%fused_computation.17 | loop fusion | flops 25164288 | bytes 25182208 | tf_op jit(solution)/shard_map/cond/branch_1_fun/reduce_sum | solution.py:76
  320.0 11.8 %fusion.17 = f32[3,512,128]{2,1,0:T(8,128)} fusion(bf16[4096,3,128]{0,2,1:T(8,128)(2,1)S(1)} %bitcast.91, f32[3,512,4096]{2,1,0:T(8,128)} %get-tuple-element.127, f32[3,512]{1,0:T(4,128)S(1)} %max.5, pred[4096]{0:T(1024)(128)(4,1)S(1)} %broadcast_compare_fusion.1, f32[3,512,128]{2,1,0:T(8,128)S(1)} %get-tuple-element.60, f32[3,512]{1,0:T(4,128)S(1)} %get-tuple-element.119), kind=kOutput, calls=%fused_computation.20 | convolution fusion | flops 1636171776 | bytes 29900800 | tf_op jit(solution)/shard_map/cond/branch_1_fun/hqk,khd->hqd/dot_general | solution.py:77
  331.8 1.4 copy.62
  333.2 0.9 copy-done.3
  334.1 1.2 broadcast_divide_fusion
  336.1 1.7 collective-permute-done
  337.8 3.8 fusion.54
  341.7 0.9 dynamic-slice_reduce_fusion
  342.6 36.0 %reduce-scatter.2.cloned.1.call-done = f32[128,1536]{1,0:T(8,128)} async-done(((f32[512,1536]{1,0:T(8,128)}), f32[128,1536]{1,0:T(8,128)}) %reduce-scatter.2.cloned.1.call-update) | async-done | bytes 786448 | tf_op jit(solution)/shard_map/reduce_scatter | solution.py:130
  378.6 1.9 multiply_convert_fusion
  (35 shorter events, 0.6 us)
Async XLA Ops:
  6.5 331.3 %copy-start = (bf16[384,3072]{1,0:T(8,128)(2,1)S(1)}, bf16[384,3072]{1,0:T(8,128)(2,1)}, u32[]{:S(2)}) copy-start(bf16[384,3072]{1,0:T(8,128)(2,1)} %param.18) | copy-start | bytes 7077892
  6.5 9.6 %copy-start.1 = (bf16[1,64,3072]{2,1,0:T(8,128)(2,1)S(1)}, bf16[1,64,3072]{2,1,0:T(8,128)(2,1)}, u32[]{:S(2)}) copy-start(bf16[1,64,3072]{2,1,0:T(8,128)(2,1)} %param.14) | copy-start | bytes 1179652
  6.5 49.1 %all-gather.5.cloned.1.call-start = ((), (), s32[]{:S(2)}) async-start(), calls=%async_computation.2 | async-start | bytes 3932160 | tf_op jit(solution)/shard_map/all_gather | solution.py:44
  13.6 81.1 %all-gather.7.cloned.1.call-start = ((), (), s32[]{:S(2)}) async-start(), calls=%async_computation.3 | async-start | bytes 1966080 | tf_op jit(solution)/shard_map/all_gather | solution.py:51
  17.1 176.7 %all-gather.9.cloned.1.call-start = ((), (), s32[]{:S(2)}) async-start(), calls=%async_computation.4 | async-start | bytes 7077888 | tf_op jit(solution)/shard_map/all_gather | solution.py:94
  63.5 1.0 copy-start.2
  65.5 228.4 %all-gather.11.cloned.1.call-start = ((), (), s32[]{:S(2)}) async-start(), calls=%async_computation.5 | async-start | bytes 7077888 | tf_op jit(solution)/shard_map/all_gather | solution.py:106
  94.1 284.5 %reduce-scatter.2.cloned.1.call-start = ((), (), s32[]{:S(2)}) async-start(), calls=%async_computation.6 | async-start | bytes 3932160 | tf_op jit(solution)/shard_map/reduce_scatter | solution.py:130
  105.2 3.0 copy-start.5
  105.2 3.0 copy-start.6
  333.2 0.9 copy-start.3
  335.3 2.5 collective-permute-start
Sparse Core Ops, SparseCore 0:
  13.8 41.8 all-gather.4
  57.3 34.9 all-gather.6
  94.5 99.2 all-gather.8
  195.8 98.0 all-gather.10
  341.8 36.7 reduce-scatter.1
where the time goes:
time: 389 us; the launch traced here: 387 us
  waiting for transfers between devices  223 us (57%)
  matrix products  63.4 us (16%)
  other arithmetic  38.5 us (10%)
  blocking collectives  24.4 us (6%)
  local copies, waits for them, and re-layouts  22.4 us (6%)
  between operations  14.8 us (4%)
    all_gather x1, waiting for transfers between devices, local(): shard_piece = lax.all_gather(fresh_pair, 'pipe', axis=1, tiled=True)  84 us
    all_gather x1, waiting for transfers between devices, local(): add_shard_piece = lax.all_gather(stale_heads, 'pipe', axis=1, tiled=True)  62.8 us
    all_gather x1, waiting for transfers between devices, local(): lax.all_gather(modulated, 'seq', axis=0, tiled=True)  38.5 us
    reduce_scatter x1, waiting for transfers between devices, local(): lax.psum_scatter(jnp.dot(mixed, w_half, preferred_element_type=jnp.float3...  36 us
    all_to_all x1, blocking collectives, local(): lax.all_to_all(stale_kv[0], 'seq', split_axis=2, concat_axis=1, tiled=True)  24.4 us
    dot_general x3, matrix products, absorb(): jnp.einsum('hqk,khd->hqd', weights.astype(jnp.bfloat16), value_rows, pref...  24.1 us
    reduce_sum x3, other arithmetic, absorb(): totals = totals * correction + jnp.sum(weights, axis=-1)  23.7 us
    dot_general x3, matrix products, absorb(): jnp.einsum('qhd,khd->hqk', queries, key_rows, preferred_element_type=jnp....  23.5 us
  transfers between devices with their start and end apart: 6, of which 5 were waited for; matrix products, arithmetic and copies ran while one was open for 18% of the time, Pallas kernels for 0%

commit v1 on v0

v1 whole, which is shorter than its diff:
```python
import math

import jax
import jax.numpy as jnp
from jax import lax
from jax.experimental import pallas as pl
from jax.experimental.pallas import tpu as pltpu
from jax.sharding import PartitionSpec as P

MESH = pl.DeviceIdType.MESH
HEAD = 128
BF16 = jnp.bfloat16
F32 = jnp.float32


def normalized(rows):
    center = rows - jnp.mean(rows, axis=-1, keepdims=True)
    spread = jnp.mean(center * center, axis=-1, keepdims=True)
    return center * lax.rsqrt(spread + 1e-06)


def kernel(
    img_in, prm_in, stale_in, wqkv_in, wpr_in, wout_in, table_in, step_in, guide_in,
    out_ref,
    img, table, prm, wqkv, wpr, wout, modbuf, prb, pkv, sbuf, kv, q, acc, top, att, peer, mix, mixall,
    lsem, st_s, st_r, m_s, m_r, mf_s, mf_r, pr_s, pr_r, pk_s, pk_r, w_s, w_r, wf_s, wf_r, ss, rs,
    a_s, a_r, x_s, x_r,
):
    dp, cfg, pipe, seq = (lax.axis_index(name) for name in ("dp", "cfg", "pipe", "seq"))
    x, zh = pipe % 4, pipe // 4
    heads, width = q.shape[0], kv.shape[-1]
    out_half = wout.shape[-1]
    model = img.shape[-1]
    scale = math.log2(math.e) / math.sqrt(HEAD)

    def at_seq(d):
        return (dp, cfg, pipe, (seq + d) % 4)

    def at_x(d):
        return (dp, cfg, zh * 4 + (x + d) % 4, seq)

    at_z = (dp, cfg, (1 - zh) * 4 + x, seq)
    at_core = (dp, 1 - cfg, pipe, seq)

    def remote(src, dst, s, r, device):
        return pltpu.make_async_remote_copy(
            src_ref=src, dst_ref=dst, send_sem=s, recv_sem=r, device_id=device, device_id_type=MESH
        )

    barrier = pltpu.get_barrier_semaphore()
    partners = [at_seq(1), at_seq(3), at_seq(2), at_x(1), at_x(3), at_x(2), at_z, at_core]
    for device in partners:
        pl.semaphore_signal(barrier, inc=1, device_id=device, device_id_type=MESH)

    half_cols = pl.ds(pl.multiple_of(cfg * out_half, 128), out_half)

    def seq_cols(d):
        return pl.ds(pl.multiple_of((seq + d) % 4 * width, 128), width)

    loads = [
        pltpu.make_async_copy(img_in.at[0], img, lsem.at[0]),
        pltpu.make_async_copy(table_in, table, lsem.at[1]),
        pltpu.make_async_copy(prm_in.at[0, pl.ds(pl.multiple_of(x * 16, 16), 16)], prm, lsem.at[2]),
        pltpu.make_async_copy(wqkv_in, wqkv, lsem.at[3]),
        pltpu.make_async_copy(stale_in.at[0, :, :, seq_cols(0)], sbuf.at[seq], lsem.at[4]),
        pltpu.make_async_copy(wpr_in, wpr, lsem.at[5]),
        pltpu.make_async_copy(wout_in.at[:, half_cols], wout.at[seq], lsem.at[6]),
    ]
    for load in loads:
        load.start()

    now = step_in[0]
    loads[0].wait()
    loads[1].wait()

    def modulate(first, count):
        def rows16(i, carry):
            rows = pl.ds(pl.multiple_of(first + i * 16, 16), 16)
            shift, gain = table[now, 0:1, :], table[now, 1:2, :]
            values = normalized(img[rows, :].astype(F32)) * (1.0 + gain) + shift
            modbuf[seq, rows, :] = values.astype(BF16)
            return carry

        lax.fori_loop(0, count // 16, rows16, 0)

    modulate(0, 64)
    pl.semaphore_wait(barrier, len(partners))

    stale_out = [
        remote(stale_in.at[0, :, :, seq_cols(d)], sbuf.at[seq], st_s.at[d - 1], st_r.at[seq], at_seq(d))
        for d in (1, 3, 2)
    ]
    for copy in stale_out:
        copy.start()

    def mod_copy(direction, half):
        part = modbuf.at[seq, pl.ds(half * 64, 64)]
        return remote(part, part, m_s.at[direction, half], m_r.at[direction, half], at_seq(1 if direction == 0 else 3))

    mod_out = [[mod_copy(a, b) for b in range(2)] for a in range(2)]
    mod_out[0][0].start()
    modulate(64, 64)
    mod_out[1][1].start()
    mod_out[0][1].start()
    mod_out[1][0].start()

    def mod_arrival(direction, half):
        part = modbuf.at[(seq + (3 if direction == 0 else 1)) % 4, pl.ds(half * 64, 64)]
        return remote(part, part, m_s.at[direction, half], m_r.at[direction, half], at_seq(1))

    def mod_forward(direction):
        part = modbuf.at[(seq + (3 if direction == 0 else 1)) % 4, pl.ds(direction * 64, 64)]
        return remote(part, part, mf_s.at[direction], mf_r.at[direction], at_seq(1 if direction == 0 else 3))

    def mod_forward_arrival(direction):
        part = modbuf.at[(seq + 2) % 4, pl.ds(direction * 64, 64)]
        return remote(part, part, mf_s.at[direction], mf_r.at[direction], at_seq(1))

    loads[2].wait()
    prb[seq] = normalized(prm[...].astype(F32)).astype(BF16)
    prompt_out = [
        remote(prb.at[seq], prb.at[seq], pr_s.at[d - 1], pr_r.at[seq], at_seq(d)) for d in (1, 3, 2)
    ]
    for copy in prompt_out:
        copy.start()

    def chunk_of(k):
        return (seq + (0, 3, 1, 2)[k]) % 4

    def piece(source, slot, k, lane, device):
        c = chunk_of(k)
        return remote(source, kv.at[slot, c], ss.at[lane, c], rs.at[slot, c], device)

    def own_copies(k, fresh):
        source = kv.at[pipe, chunk_of(k)] if fresh else sbuf.at[chunk_of(k)]
        return (
            (x < 3 if fresh else x == 3, piece(source, pipe, k, 0, at_x(1))),
            (x == 0 if fresh else x > 0, piece(source, pipe, k, 1, at_x(3))),
            (zh == 0 if fresh else zh == 1, piece(source, pipe, k, 2, at_z)),
        )

    def send_own(k, fresh):
        for condition, copy in own_copies(k, fresh):
            pl.when(condition)(copy.start)

    def slot_in(d):
        return zh * 4 + (x + d) % 4

    def slot_far(d):
        return (1 - zh) * 4 + (x + d) % 4

    def landed(slot, k):
        here = kv.at[slot, chunk_of(k)]
        remote(here, here, ss.at[0, 0], rs.at[slot, chunk_of(k)], at_x(1)).wait_recv()

    def pass_on(slot, k, lane, device):
        return piece(kv.at[slot, chunk_of(k)], slot, k, lane, device)

    def any_of(places):
        found = x == places[0]
        for place in places[1:]:
            found = found | (x == place)
        return found

    IN_PLUS = ((1, 2), (0, 2))
    IN_MINUS = ((1, 2), (1, 3))
    FAR_PLUS = ((1, 3), (0, 3))
    FAR_MINUS = ((0, 2), (0, 3))

    def spread_far(k):
        return (pass_on(slot_far(0), k, 3, at_x(1)), pass_on(slot_far(0), k, 4, at_x(3)))

    def forward(which, k):
        places = (IN_PLUS, IN_MINUS, FAR_PLUS, FAR_MINUS)[which][k % 2]
        slot = (slot_in(3), slot_in(1), slot_far(3), slot_far(1))[which]
        return any_of(places), pass_on(slot, k, 5 + which, at_x((1, 3, 1, 3)[which]))

    def serve_z(k):
        landed(slot_far(0), k)
        for copy in spread_far(k):
            copy.start()

    def serve(which, k):
        landed((slot_in(3), slot_in(1), slot_far(3), slot_far(1))[which], k)
        condition, copy = forward(which, k)
        pl.when(condition)(copy.start)

    def when(condition, action, *arguments):
        @pl.when(condition)
        def _():
            action(*arguments)

    def late_one(k):
        when(zh == 1, serve_z, k)
        when(x > 0, serve, 0, k)
        when(x == 3, serve, 1, k)

    def late_two(k):
        when(zh == 1, serve, 2, k)
        when(zh == 1, serve, 3, k)

    def project(k):
        c = chunk_of(k)
        rows = modbuf[c]
        for j in (1, 2):
            kv[pipe, c, j - 1] = jnp.dot(rows, wqkv[j], preferred_element_type=F32).astype(BF16)
        send_own(k, True)
        block = jnp.dot(rows, wqkv[0], preferred_element_type=F32).astype(BF16)
        place = pl.ds(pl.multiple_of(c * 128, 128), 128)
        for h in range(heads):
            q[h, place, :] = block[:, h * HEAD : (h + 1) * HEAD]

    loads[3].wait()
    project(0)

    loads[4].wait()
    for d in (1, 3, 2):
        c = (seq + d) % 4
        remote(sbuf.at[c], sbuf.at[c], st_s.at[0], st_r.at[c], at_seq(1)).wait_recv()
    for k in range(4):
        send_own(k, False)

    mod_arrival(0, 0).wait_recv()
    mod_forward(0).start()
    mod_arrival(1, 1).wait_recv()
    mod_forward(1).start()

    loads[5].wait()
    for d in (1, 3, 2):
        c = (seq + d) % 4
        remote(prb.at[c], prb.at[c], pr_s.at[0], pr_r.at[c], at_seq(1)).wait_recv()
    prompt_rows = prb[...].reshape(64, model)
    for j in range(2):
        pkv[x, j] = jnp.dot(prompt_rows, wpr[j], preferred_element_type=F32).astype(BF16)
    pkv_out = [remote(pkv.at[x], pkv.at[x], pk_s.at[d - 1], pk_r.at[x], at_x(d)) for d in (1, 3, 2)]
    for copy in pkv_out:
        copy.start()

    late_one(0)

    mod_arrival(0, 1).wait_recv()
    project(1)
    late_two(0)
    mod_arrival(1, 0).wait_recv()
    project(2)

    loads[6].wait()
    wout_out = [
        remote(wout.at[seq], wout.at[seq], w_s.at[a], w_r.at[a], at_seq(1 if a == 0 else 3)) for a in range(2)
    ]
    for copy in wout_out:
        copy.start()

    for k in range(4):
        when(zh == 0, serve_z, k)
        when(x == 0, serve, 0, k)
        when(x < 3, serve, 1, k)

    late_one(1)
    for direction in range(2):
        mod_forward_arrival(direction).wait_recv()
    project(3)

    late_two(1)
    late_one(2)
    for k in range(4):
        when(zh == 0, serve, 2, k)
        when(zh == 0, serve, 3, k)

    def attend(keys_of, values_of, first):
        def one_head(h, carry):
            lanes = pl.ds(pl.multiple_of(h * HEAD, HEAD), HEAD)
            keys = keys_of(lanes)
            values = values_of(lanes)
            values = jnp.concatenate([values, jnp.ones_like(values)], axis=1)
            scores = lax.dot_general(q[h], keys, (((1,), (1,)), ((), ())), preferred_element_type=F32)
            peak = jnp.max(scores, axis=1, keepdims=True)
            if first:
                new_top = peak
            else:
                old_top = top[h][:, :1]
                new_top = jnp.maximum(old_top, peak)
            weights = jnp.exp2(scores * scale - new_top * scale).astype(BF16)
            part = jnp.dot(weights, values, preferred_element_type=F32)
            if first:
                acc[h] = part
            else:
                acc[h] = acc[h] * jnp.exp2((old_top - new_top) * scale) + part
            top[h] = jnp.broadcast_to(new_top, top.shape[1:])
            return carry

        lax.fori_loop(0, heads, one_head, 0)

    def attend_slot(slot):
        attend(
            lambda lanes: kv[slot, :, 0, :, lanes].reshape(512, HEAD),
            lambda lanes: kv[slot, :, 1, :, lanes].reshape(512, HEAD),
            False,
        )

    for d in (1, 3, 2):
        c = (x + d) % 4
        remote(pkv.at[c], pkv.at[c], pk_s.at[0], pk_r.at[c], at_x(1)).wait_recv()
    attend(
        lambda lanes: pkv[:, 0, :, lanes].reshape(256, HEAD),
        lambda lanes: pkv[:, 1, :, lanes].reshape(256, HEAD),
        True,
    )
    late_two(2)
    late_one(3)
    attend_slot(pipe)
    late_two(3)
    attend_slot(slot_in(3))
    attend_slot(slot_in(1))
    attend_slot(slot_far(0))

    def wout_arrival(direction):
        part = wout.at[(seq + (3 if direction == 0 else 1)) % 4]
        return remote(part, part, w_s.at[direction], w_r.at[direction], at_seq(1))

    def wout_forward(direction, source):
        part = wout.at[source, pl.ds(direction * (width // 2), width // 2)]
        return remote(part, part, wf_s.at[direction], wf_r.at[direction], at_seq(1 if direction == 0 else 3))

    wout_pass = []
    for direction in range(2):
        wout_arrival(direction).wait_recv()
        copy = wout_forward(direction, (seq + (3 if direction == 0 else 1)) % 4)
        copy.start()
        wout_pass.append(copy)

    attend_slot(slot_far(3))
    attend_slot(slot_far(1))
    for k in range(4):
        landed(slot_in(2), k)
    attend_slot(slot_in(2))
    for k in range(4):
        landed(slot_far(2), k)
    attend_slot(slot_far(2))

    att_out = []
    for h in range(heads):
        block = acc[h]
        att[h] = block[:, :HEAD] / block[:, HEAD : HEAD + 1]
        copy = remote(att.at[h], peer.at[h], a_s.at[h], a_r.at[h], at_core)
        copy.start()
        att_out.append(copy)
    guide = guide_in[0]
    first_side = cfg == 0
    for h in range(heads):
        att_out[h].wait_recv()
        mine, other = att[h], peer[h]
        cond_part = jnp.where(first_side, mine, other)
        uncond = jnp.where(first_side, other, mine)
        mixed = (uncond + guide * (cond_part - uncond)).astype(BF16)
        mix[:, :, h * HEAD : (h + 1) * HEAD] = mixed.reshape(4, 128, HEAD)
    mix_out = [
        remote(mix.at[(seq + d) % 4], mixall.at[seq], x_s.at[d - 1], x_r.at[seq], at_seq(d)) for d in (2, 1, 3)
    ]
    for copy in mix_out:
        copy.start()
    total = jnp.dot(mix[seq], wout[seq], preferred_element_type=F32)
    for direction in range(2):
        wout_forward(direction, (seq + 2) % 4).wait_recv()
    for d in (1, 3, 2):
        c = (seq + d) % 4
        remote(mixall.at[c], mixall.at[c], x_s.at[0], x_r.at[c], at_seq(1)).wait_recv()
        total = total + jnp.dot(mixall[c], wout[c], preferred_element_type=F32)
    out_ref[...] = (table[now, 2:3, half_cols] * total).astype(BF16)

    for copy in stale_out + mod_out[0] + mod_out[1] + prompt_out + pkv_out + wout_out + wout_pass + att_out + mix_out:
        copy.wait_send()
    for direction in range(2):
        mod_forward(direction).wait_send()
    for k in range(4):
        for lane in range(3):
            piece(sbuf.at[chunk_of(k)], pipe, k, lane, at_x(1)).wait_send()
        for copy in spread_far(k):
            copy.wait_send()
        for which in range(4):
            condition, copy = forward(which, k)
            pl.when(condition)(copy.wait_send)


def local(
    image_states, prompt_states, stale_kv, w_image_qkv, w_prompt_kv, w_output, mod_table, timestep, guidance
):
    rows, model = image_states.shape[1:]
    width = w_output.shape[0]
    heads = width // HEAD
    half = w_output.shape[1] // 2
    dma = pltpu.SemaphoreType.DMA
    anywhere = pl.BlockSpec(memory_space=pl.ANY)
    scalar = pl.BlockSpec(memory_space=pltpu.SMEM)
    return pl.pallas_call(
        kernel,
        out_shape=jax.ShapeDtypeStruct((rows, half), BF16),
        in_specs=[anywhere] * 7 + [scalar] * 2,
        out_specs=pl.BlockSpec(memory_space=pltpu.VMEM),
        scratch_shapes=[
            pltpu.VMEM((rows, model), BF16),
            pltpu.VMEM(mod_table.shape, F32),
            pltpu.VMEM((16, model), BF16),
            pltpu.VMEM(w_image_qkv.shape, BF16),
            pltpu.VMEM(w_prompt_kv.shape, BF16),
            pltpu.VMEM((4, width, half), BF16),
            pltpu.VMEM((4, rows, model), BF16),
            pltpu.VMEM((4, 16, model), BF16),
            pltpu.VMEM((4, 2, 64, width), BF16),
            pltpu.VMEM((4, 2, rows, width), BF16),
            pltpu.VMEM((8, 4, 2, rows, width), BF16),
            pltpu.VMEM((heads, 4 * rows, HEAD), BF16),
            pltpu.VMEM((heads, 4 * rows, 2 * HEAD), F32),
            pltpu.VMEM((heads, 4 * rows, HEAD), F32),
            pltpu.VMEM((heads, 4 * rows, HEAD), F32),
            pltpu.VMEM((heads, 4 * rows, HEAD), F32),
            pltpu.VMEM((4, rows, width), BF16),
            pltpu.VMEM((4, rows, width), BF16),
            dma((7,)), dma((3,)), dma((4,)), dma((2, 2)), dma((2, 2)), dma((2,)), dma((2,)),
            dma((3,)), dma((4,)), dma((3,)), dma((4,)), dma((2,)), dma((2,)), dma((2,)), dma((2,)),
            dma((9, 4)), dma((8, 4)), dma((heads,)), dma((heads,)), dma((3,)), dma((4,)),
        ],
        compiler_params=pltpu.CompilerParams(
            collective_id=0, has_side_effects=True, vmem_limit_bytes=58 * 2**20
        ),
        name="guided_attention",
    )(image_states, prompt_states, stale_kv, w_image_qkv, w_prompt_kv, w_output, mod_table, timestep, guidance)


def solution(mesh):
    return jax.shard_map(
        local,
        mesh=mesh,
        in_specs=(
            P("cfg", ("dp", "pipe", "seq"), None),
            P("cfg", ("dp", "seq"), None),
            P("cfg", None, ("dp", "pipe", "seq"), None),
            P(None, None, "seq"),
            P(None, None, "seq"),
            P("seq", None),
            P(),
            P("dp"),
            P("dp"),
        ),
        out_specs=P(("dp", "pipe", "seq"), "cfg"),
        check_vma=False,
    )
```

time: 389 us -> 133 us (0.34)
  the two profiles are of different devices: /device:TPU:6 before, /device:TPU:65 now
where the time goes in v1:
time: 133 us
  Pallas kernels  126 us (95%)
  local copies, waits for them, and re-layouts  6.06 us (5%)
    pallas_call x1, Pallas kernels, local(): pl.pallas_call(kernel, out_shape=jax.ShapeDtypeStruct((rows, half), BF16)...  126 us
    unnamed x2, local copies, waits for them, and re-layouts  6.06 us

profile of v1, /device:TPU:65, one launch (start us, length us, event | category | flops | bytes accessed | tf_op | source)
XLA Modules:
  0.0 133.1 jit_solution(8994527903117470942)
XLA Ops:
  1.3 4.3 %copy.10.table_in = f32[50,3,3072]{2,1,0:T(4,128)} copy(f32[50,3,3072]{2,0,1:T(8,128)} %param.15) | data formatting | bytes 3686400 | tf_op args[6]
  5.6 125.8 %guided_attention.1 = bf16[128,1536]{1,0:T(8,128)(2,1)} custom-call(bf16[1,128,3072]{2,1,0:T(8,128)(2,1)} %img_in.1, bf16[1,64,3072]{2,1,0:T(8,128)(2,1)} %prm_in.1, bf16[1,2,128,1536]{3,2,1,0:T(8,128)(2,1)} %stale_in.1, bf16[3,3072,384]{2,1,0:T(8,128)(2,1)} %wqkv_in.1, bf16[2,3072,384]{2,1,0:T(8,128)(2,1)} %wpr_in.1, bf16[384,3072]{1,0:T(8,128)(2,1)} %wout_in.1, ...), custom_call_target="tpu_custom_call" | custom-call | tf_op jit(solution)/shard_map/guided_attention/pallas_call | solution.py:395
  131.4 1.8 %copy.14 = bf16[128,1536]{1,0:T(8,128)(2,1)} copy(bf16[128,1536]{1,0:T(8,128)(2,1)} %guided_attention.1) | data formatting | bytes 786432

commit v2 on v1

--- a/solution.py
+++ b/solution.py
@@ -76,9 +76,9 @@
     def modulate(first, count):
         def rows16(i, carry):
             rows = pl.ds(pl.multiple_of(first + i * 16, 16), 16)
-            shift, gain = table[now, 0:1, :], table[now, 1:2, :]
+            shift, gain = table[0, pl.ds(now, 1), :], table[1, pl.ds(now, 1), :]
             values = normalized(img[rows, :].astype(F32)) * (1.0 + gain) + shift
-            modbuf[seq, rows, :] = values.astype(BF16)
+            modbuf[0, rows, :] = values.astype(BF16)
             return carry
 
         lax.fori_loop(0, count // 16, rows16, 0)
@@ -88,51 +88,35 @@
 
     stale_out = [
         remote(stale_in.at[0, :, :, seq_cols(d)], sbuf.at[seq], st_s.at[d - 1], st_r.at[seq], at_seq(d))
-        for d in (1, 3, 2)
+        for d in (2, 1, 3)
     ]
     for copy in stale_out:
         copy.start()
-
-    def mod_copy(direction, half):
-        part = modbuf.at[seq, pl.ds(half * 64, 64)]
-        return remote(part, part, m_s.at[direction, half], m_r.at[direction, half], at_seq(1 if direction == 0 else 3))
+    modulate(64, 64)
+
+    def half_rows(half):
+        return pl.ds(half * 64, 64)
+
+    def mod_copy(direction, order):
+        half = direction if order == 0 else 1 - direction
+        source = modbuf.at[0, half_rows(half)]
+        target = modbuf.at[1 + order, half_rows(direction)]
+        return remote(
+            source, target, m_s.at[direction, order], m_r.at[direction, order], at_seq(1 if direction == 0 else 3)
+        )
+
+    def mod_forward(direction):
+        source = modbuf.at[1, half_rows(direction)]
+        target = modbuf.at[3, half_rows(direction)]
+        return remote(source, target, mf_s.at[direction], mf_r.at[direction], at_seq(1 if direction == 0 else 3))
 
     mod_out = [[mod_copy(a, b) for b in range(2)] for a in range(2)]
-    mod_out[0][0].start()
-    modulate(64, 64)
-    mod_out[1][1].start()
-    mod_out[0][1].start()
-    mod_out[1][0].start()
-
-    def mod_arrival(direction, half):
-        part = modbuf.at[(seq + (3 if direction == 0 else 1)) % 4, pl.ds(half * 64, 64)]
-        return remote(part, part, m_s.at[direction, half], m_r.at[direction, half], at_seq(1))
-
-    def mod_forward(direction):
-        part = modbuf.at[(seq + (3 if direction == 0 else 1)) % 4, pl.ds(direction * 64, 64)]
-        return remote(part, part, mf_s.at[direction], mf_r.at[direction], at_seq(1 if direction == 0 else 3))
-
-    def mod_forward_arrival(direction):
-        part = modbuf.at[(seq + 2) % 4, pl.ds(direction * 64, 64)]
-        return remote(part, part, mf_s.at[direction], mf_r.at[direction], at_seq(1))
-
-    loads[2].wait()
-    prb[seq] = normalized(prm[...].astype(F32)).astype(BF16)
-    prompt_out = [
-        remote(prb.at[seq], prb.at[seq], pr_s.at[d - 1], pr_r.at[seq], at_seq(d)) for d in (1, 3, 2)
-    ]
-    for copy in prompt_out:
-        copy.start()
-
-    def chunk_of(k):
-        return (seq + (0, 3, 1, 2)[k]) % 4
 
     def piece(source, slot, k, lane, device):
-        c = chunk_of(k)
-        return remote(source, kv.at[slot, c], ss.at[lane, c], rs.at[slot, c], device)
+        return remote(source, kv.at[slot, k], ss.at[lane, k], rs.at[slot, k], device)
 
     def own_copies(k, fresh):
-        source = kv.at[pipe, chunk_of(k)] if fresh else sbuf.at[chunk_of(k)]
+        source = kv.at[pipe, k] if fresh else sbuf.at[k]
         return (
             (x < 3 if fresh else x == 3, piece(source, pipe, k, 0, at_x(1))),
             (x == 0 if fresh else x > 0, piece(source, pipe, k, 1, at_x(3))),
@@ -150,11 +134,11 @@
         return (1 - zh) * 4 + (x + d) % 4
 
     def landed(slot, k):
-        here = kv.at[slot, chunk_of(k)]
-        remote(here, here, ss.at[0, 0], rs.at[slot, chunk_of(k)], at_x(1)).wait_recv()
+        here = kv.at[slot, k]
+        remote(here, here, ss.at[0, 0], rs.at[slot, k], at_x(1)).wait_recv()
 
     def pass_on(slot, k, lane, device):
-        return piece(kv.at[slot, chunk_of(k)], slot, k, lane, device)
+        return piece(kv.at[slot, k], slot, k, lane, device)
 
     def any_of(places):
         found = x == places[0]
@@ -200,15 +184,36 @@
         when(zh == 1, serve, 3, k)
 
     def project(k):
-        c = chunk_of(k)
-        rows = modbuf[c]
+        rows = modbuf[k]
         for j in (1, 2):
-            kv[pipe, c, j - 1] = jnp.dot(rows, wqkv[j], preferred_element_type=F32).astype(BF16)
+            kv[pipe, k, j - 1] = jnp.dot(rows, wqkv[j], preferred_element_type=F32).astype(BF16)
         send_own(k, True)
         block = jnp.dot(rows, wqkv[0], preferred_element_type=F32).astype(BF16)
-        place = pl.ds(pl.multiple_of(c * 128, 128), 128)
         for h in range(heads):
-            q[h, place, :] = block[:, h * HEAD : (h + 1) * HEAD]
+            q[h, k * 128 : (k + 1) * 128, :] = block[:, h * HEAD : (h + 1) * HEAD]
+
+    def early_far(k):
+        when(zh == 0, serve_z, k)
+
+    def early_in(k):
+        when(x == 0, serve, 0, k)
+        when(x < 3, serve, 1, k)
+
+    def early_far_two(k):
+        when(zh == 0, serve, 2, k)
+        when(zh == 0, serve, 3, k)
+
+    def mod_arrived(order):
+        for direction in range(2):
+            mod_out[direction][order].wait_recv()
+            if order == 0:
+                mod_forward(direction).start()
+
+    for copy in stale_out:
+        copy.wait_send()
+    for order in range(2):
+        for direction in range(2):
+            mod_out[direction][order].start()
 
     loads[3].wait()
     project(0)
@@ -220,10 +225,45 @@
     for k in range(4):
         send_own(k, False)
 
-    mod_arrival(0, 0).wait_recv()
-    mod_forward(0).start()
-    mod_arrival(1, 1).wait_recv()
-    mod_forward(1).start()
+    loads[2].wait()
+    prb[seq] = normalized(prm[...].astype(F32)).astype(BF16)
+
+    late_one(0)
+    early_far(0)
+    mod_arrived(0)
+    project(1)
+    late_two(0)
+    early_far(1)
+    early_in(0)
+    early_in(1)
+
+    mod_arrived(1)
+    prompt_out = [
+        remote(prb.at[seq], prb.at[seq], pr_s.at[d - 1], pr_r.at[seq], at_seq(d)) for d in (1, 3, 2)
+    ]
+    for copy in prompt_out:
+        copy.start()
+    project(2)
+
+    loads[6].wait()
+    wout_out = [
+        remote(wout.at[seq], wout.at[seq], w_s.at[a], w_r.at[a], at_seq(1 if a == 0 else 3)) for a in range(2)
+    ]
+    for copy in wout_out:
+        copy.start()
+
+    late_one(1)
+    early_far(2)
+    early_far(3)
+    early_in(2)
+    early_in(3)
+    early_far_two(0)
+    early_far_two(1)
+    for direction in range(2):
+        mod_forward(direction).wait_recv()
+    project(3)
+    late_two(1)
+    late_one(2)
 
     loads[5].wait()
     for d in (1, 3, 2):
@@ -236,36 +276,10 @@
     for copy in pkv_out:
         copy.start()
 
-    late_one(0)
-
-    mod_arrival(0, 1).wait_recv()
-    project(1)
-    late_two(0)
-    mod_arrival(1, 0).wait_recv()
-    project(2)
-
-    loads[6].wait()
-    wout_out = [
-        remote(wout.at[seq], wout.at[seq], w_s.at[a], w_r.at[a], at_seq(1 if a == 0 else 3)) for a in range(2)
-    ]
-    for copy in wout_out:
-        copy.start()
-
-    for k in range(4):
-        when(zh == 0, serve_z, k)
-        when(x == 0, serve, 0, k)
-        when(x < 3, serve, 1, k)
-
-    late_one(1)
-    for direction in range(2):
-        mod_forward_arrival(direction).wait_recv()
-    project(3)
-
-    late_two(1)
-    late_one(2)
-    for k in range(4):
-        when(zh == 0, serve, 2, k)
-        when(zh == 0, serve, 3, k)
+    early_far_two(2)
+    early_far_two(3)
+    late_two(2)
+    late_one(3)
 
     def attend(keys_of, values_of, first):
         def one_head(h, carry):
@@ -291,25 +305,23 @@
 
         lax.fori_loop(0, heads, one_head, 0)
 
-    def attend_slot(slot):
+    def attend_slot(slot, first=False):
         attend(
             lambda lanes: kv[slot, :, 0, :, lanes].reshape(512, HEAD),
             lambda lanes: kv[slot, :, 1, :, lanes].reshape(512, HEAD),
-            False,
+            first,
         )
 
+    attend_slot(pipe, True)
+    late_two(3)
     for d in (1, 3, 2):
         c = (x + d) % 4
         remote(pkv.at[c], pkv.at[c], pk_s.at[0], pk_r.at[c], at_x(1)).wait_recv()
     attend(
         lambda lanes: pkv[:, 0, :, lanes].reshape(256, HEAD),
         lambda lanes: pkv[:, 1, :, lanes].reshape(256, HEAD),
-        True,
+        False,
     )
-    late_two(2)
-    late_one(3)
-    attend_slot(pipe)
-    late_two(3)
     attend_slot(slot_in(3))
     attend_slot(slot_in(1))
     attend_slot(slot_far(0))
@@ -353,28 +365,31 @@
         cond_part = jnp.where(first_side, mine, other)
         uncond = jnp.where(first_side, other, mine)
         mixed = (uncond + guide * (cond_part - uncond)).astype(BF16)
-        mix[:, :, h * HEAD : (h + 1) * HEAD] = mixed.reshape(4, 128, HEAD)
+        mix[:, :, :, h * HEAD : (h + 1) * HEAD] = mixed.reshape(4, 2, 64, HEAD)
     mix_out = [
-        remote(mix.at[(seq + d) % 4], mixall.at[seq], x_s.at[d - 1], x_r.at[seq], at_seq(d)) for d in (2, 1, 3)
+        remote(mix.at[group, part], mixall.at[seq, half], x_s.at[d - 1, half], x_r.at[seq, half], at_seq(d))
+        for d, half, group, part in ((2, 0, 3, 0), (2, 1, 3, 1), (1, 0, 2, 1), (1, 1, 1, 1), (3, 0, 1, 0), (3, 1, 2, 0))
     ]
     for copy in mix_out:
         copy.start()
-    total = jnp.dot(mix[seq], wout[seq], preferred_element_type=F32)
+    total = jnp.dot(mix[0].reshape(128, width), wout[seq], preferred_element_type=F32)
     for direction in range(2):
         wout_forward(direction, (seq + 2) % 4).wait_recv()
     for d in (1, 3, 2):
         c = (seq + d) % 4
-        remote(mixall.at[c], mixall.at[c], x_s.at[0], x_r.at[c], at_seq(1)).wait_recv()
-        total = total + jnp.dot(mixall[c], wout[c], preferred_element_type=F32)
-    out_ref[...] = (table[now, 2:3, half_cols] * total).astype(BF16)
-
-    for copy in stale_out + mod_out[0] + mod_out[1] + prompt_out + pkv_out + wout_out + wout_pass + att_out + mix_out:
+        for half in range(2):
+            here = mixall.at[c, half]
+            remote(here, here, x_s.at[0, 0], x_r.at[c, half], at_seq(1)).wait_recv()
+        total = total + jnp.dot(mixall[c].reshape(128, width), wout[c], preferred_element_type=F32)
+    out_ref[...] = (table[2, pl.ds(now, 1), half_cols] * total).astype(BF16)
+
+    for copy in mod_out[0] + mod_out[1] + prompt_out + pkv_out + wout_out + wout_pass + att_out + mix_out:
         copy.wait_send()
     for direction in range(2):
         mod_forward(direction).wait_send()
     for k in range(4):
         for lane in range(3):
-            piece(sbuf.at[chunk_of(k)], pipe, k, lane, at_x(1)).wait_send()
+            piece(sbuf.at[k], pipe, k, lane, at_x(1)).wait_send()
         for copy in spread_far(k):
             copy.wait_send()
         for which in range(4):
@@ -386,6 +401,7 @@
     image_states, prompt_states, stale_kv, w_image_qkv, w_prompt_kv, w_output, mod_table, timestep, guidance
 ):
     rows, model = image_states.shape[1:]
+    table = jnp.transpose(mod_table, (1, 0, 2))
     width = w_output.shape[0]
     heads = width // HEAD
     half = w_output.shape[1] // 2
@@ -399,7 +415,7 @@
         out_specs=pl.BlockSpec(memory_space=pltpu.VMEM),
         scratch_shapes=[
             pltpu.VMEM((rows, model), BF16),
-            pltpu.VMEM(mod_table.shape, F32),
+            pltpu.VMEM(table.shape, F32),
             pltpu.VMEM((16, model), BF16),
             pltpu.VMEM(w_image_qkv.shape, BF16),
             pltpu.VMEM(w_prompt_kv.shape, BF16),
@@ -414,17 +430,17 @@
             pltpu.VMEM((heads, 4 * rows, HEAD), F32),
             pltpu.VMEM((heads, 4 * rows, HEAD), F32),
             pltpu.VMEM((heads, 4 * rows, HEAD), F32),
-            pltpu.VMEM((4, rows, width), BF16),
-            pltpu.VMEM((4, rows, width), BF16),
+            pltpu.VMEM((4, 2, rows // 2, width), BF16),
+            pltpu.VMEM((4, 2, rows // 2, width), BF16),
             dma((7,)), dma((3,)), dma((4,)), dma((2, 2)), dma((2, 2)), dma((2,)), dma((2,)),
             dma((3,)), dma((4,)), dma((3,)), dma((4,)), dma((2,)), dma((2,)), dma((2,)), dma((2,)),
-            dma((9, 4)), dma((8, 4)), dma((heads,)), dma((heads,)), dma((3,)), dma((4,)),
+            dma((9, 4)), dma((8, 4)), dma((heads,)), dma((heads,)), dma((3, 2)), dma((4, 2)),
         ],
         compiler_params=pltpu.CompilerParams(
             collective_id=0, has_side_effects=True, vmem_limit_bytes=58 * 2**20
         ),
         name="guided_attention",
-    )(image_states, prompt_states, stale_kv, w_image_qkv, w_prompt_kv, w_output, mod_table, timestep, guidance)
+    )(image_states, prompt_states, stale_kv, w_image_qkv, w_prompt_kv, w_output, table, timestep, guidance)
 
 
 def solution(mesh):

time: 133 us -> 121 us (0.910)
  the two profiles are of different devices: /device:TPU:65 before, /device:TPU:75 now
where the time goes in v2:
time: 121 us
  Pallas kernels  118 us (98%)
  local copies, waits for them, and re-layouts  1.77 us (1%)
  between operations  1.31 us (1%)
    pallas_call x1, Pallas kernels, local(): pl.pallas_call(kernel, out_shape=jax.ShapeDtypeStruct((rows, half), BF16)...  118 us

profile of v2, /device:TPU:75, one launch (start us, length us, event | category | flops | bytes accessed | tf_op | source)
XLA Modules:
  0.0 121.1 jit_solution(12640436398723836194)
XLA Ops:
  1.3 118.0 %guided_attention.1 = bf16[128,1536]{1,0:T(8,128)(2,1)} custom-call(bf16[1,128,3072]{2,1,0:T(8,128)(2,1)} %img_in.1, bf16[1,64,3072]{2,1,0:T(8,128)(2,1)} %prm_in.1, bf16[1,2,128,1536]{3,2,1,0:T(8,128)(2,1)} %stale_in.1, bf16[3,3072,384]{2,1,0:T(8,128)(2,1)} %wqkv_in.1, bf16[2,3072,384]{2,1,0:T(8,128)(2,1)} %wpr_in.1, bf16[384,3072]{1,0:T(8,128)(2,1)} %wout_in.1, ...), custom_call_target="tpu_custom_call" | custom-call | tf_op jit(solution)/shard_map/guided_attention/pallas_call | solution.py:411
  119.3 1.8 %copy.13 = bf16[128,1536]{1,0:T(8,128)(2,1)} copy(bf16[128,1536]{1,0:T(8,128)(2,1)} %guided_attention.1) | data formatting | bytes 786432

commit v3 on v2

--- a/solution.py
+++ b/solution.py
@@ -11,6 +11,54 @@
 HEAD = 128
 BF16 = jnp.bfloat16
 F32 = jnp.float32
+
+
+PLAN = (
+    ((20, 21, 22, 23, 16), (17, 18), (19, 12), (13,), (3,), (14,), (15,), (), (1,), (), ()),
+    ((20, 21, 22, 23, 0, 16, 4), (17, 5, 18, 6, 1), (19, 7), (), (2,), (14,), (), (3,), (15,), (), ()),
+    ((20, 21, 22, 23, 0, 16, 4), (17, 18, 6), (1, 12, 13), (14,), (), (2, 15), (), (19,), (3,), (), ()),
+    ((20, 21, 22, 23, 0, 16), (17, 12, 8, 5), (1, 19, 13, 9, 14), (), (2, 15), (3,), (7,), (18,), (), (), ()),
+    ((20, 21, 22, 23, 16, 4), (5, 1, 17, 6), (7, 3, 12, 8, 18), (), (), (), (9, 19), (10, 13, 11), (), (), ()),
+    ((20, 21, 22, 23, 16, 0, 4), (8, 5, 6), (9, 17, 2, 18), (), (), (19,), (7, 10), (), (11,), (), ()),
+    ((20, 21, 22, 16, 0, 4), (5, 17, 1, 6), (7, 23, 18, 2), (), (), (19,), (3,), (10,), (11,), (), ()),
+    ((20, 21, 22, 23, 16), (8, 17, 5), (18,), (9,), (19,), (), (10, 7), (), (), (11,), ()),
+)
+ATTEND = (
+    (0, 4, 1, 5, 2, 3, 6, 7),
+    (1, 5, 2, 4, 0, 6, 7, 3),
+    (2, 3, 7, 5, 6, 1, 4, 0),
+    (3, 4, 2, 0, 7, 6, 1, 5),
+    (4, 5, 7, 0, 3, 1, 6, 2),
+    (5, 7, 1, 6, 4, 0, 2, 3),
+    (6, 7, 2, 5, 3, 1, 4, 0),
+    (7, 3, 6, 4, 0, 5, 2, 1),
+)
+
+
+def passes_to(place, whence, k):
+    upper, x = divmod(place, 4)
+    if not upper:
+        x = 3 - x
+        whence = (1, 0, 3, 2, 4)[whence]
+    far = k in (2, 3)
+    ways = {
+        0: "+" if x == 2 or (x == 1 and k % 2 == 0) or (x == 0 and k % 2 == 1) else "",
+        1: ("-" if x == 1 or (x == 2 and k % 2 == 0) or (x == 3 and k % 2 == 1) else "") + ("z" if x < 3 else ""),
+        2: "+" if x != 2 or far else "",
+        3: "-" if x == 0 and not far else "",
+        4: "+-" if x == 3 else "-",
+    }[whence]
+    return ways if upper else ways.translate(str.maketrans("+-", "-+"))
+
+
+def patch_from(place, whence):
+    upper, x = divmod(place, 4)
+    d = (3, 1, 3, 1, 0)[whence]
+    return (upper if whence < 2 else 1 - upper) * 4 + (x + d) % 4
+
+
+def awaited(place, patch, k):
+    return any(patch_from(place, w) == patch and passes_to(place, w, k) for w in range(5))
 
 
 def normalized(rows):
@@ -115,89 +163,85 @@
     def piece(source, slot, k, lane, device):
         return remote(source, kv.at[slot, k], ss.at[lane, k], rs.at[slot, k], device)
 
-    def own_copies(k, fresh):
-        source = kv.at[pipe, k] if fresh else sbuf.at[k]
-        return (
-            (x < 3 if fresh else x == 3, piece(source, pipe, k, 0, at_x(1))),
-            (x == 0 if fresh else x > 0, piece(source, pipe, k, 1, at_x(3))),
-            (zh == 0 if fresh else zh == 1, piece(source, pipe, k, 2, at_z)),
-        )
-
-    def send_own(k, fresh):
-        for condition, copy in own_copies(k, fresh):
-            pl.when(condition)(copy.start)
-
-    def slot_in(d):
-        return zh * 4 + (x + d) % 4
-
-    def slot_far(d):
-        return (1 - zh) * 4 + (x + d) % 4
+    def toward(way):
+        return {"+": at_x(1), "-": at_x(3), "z": at_z}[way]
+
+    def send_own(k):
+        for condition, lane, way in ((x < 3, 0, "+"), (x == 0, 1, "-"), (zh == 0, 2, "z")):
+            pl.when(condition)(piece(kv.at[pipe, k], pipe, k, lane, toward(way)).start)
+
+    def send_stale(place, k):
+        upper, column = divmod(place, 4)
+        ways = (("+", 0),) * (column == 3) + (("-", 1),) * (column > 0) + (("z", 2),) * upper
+        for way, lane in ways:
+            piece(sbuf.at[k], place, k, lane, toward(way)).start()
 
     def landed(slot, k):
         here = kv.at[slot, k]
         remote(here, here, ss.at[0, 0], rs.at[slot, k], at_x(1)).wait_recv()
 
-    def pass_on(slot, k, lane, device):
-        return piece(kv.at[slot, k], slot, k, lane, device)
-
-    def any_of(places):
-        found = x == places[0]
-        for place in places[1:]:
-            found = found | (x == place)
-        return found
-
-    IN_PLUS = ((1, 2), (0, 2))
-    IN_MINUS = ((1, 2), (1, 3))
-    FAR_PLUS = ((1, 3), (0, 3))
-    FAR_MINUS = ((0, 2), (0, 3))
-
-    def spread_far(k):
-        return (pass_on(slot_far(0), k, 3, at_x(1)), pass_on(slot_far(0), k, 4, at_x(3)))
-
-    def forward(which, k):
-        places = (IN_PLUS, IN_MINUS, FAR_PLUS, FAR_MINUS)[which][k % 2]
-        slot = (slot_in(3), slot_in(1), slot_far(3), slot_far(1))[which]
-        return any_of(places), pass_on(slot, k, 5 + which, at_x((1, 3, 1, 3)[which]))
-
-    def serve_z(k):
-        landed(slot_far(0), k)
-        for copy in spread_far(k):
+    def passed(place, whence, k):
+        slot = patch_from(place, whence)
+        for way in passes_to(place, whence, k):
+            yield piece(kv.at[slot, k], slot, k, 3 + 3 * whence + "+-z".index(way), toward(way))
+
+    def step(place, code):
+        whence, k = divmod(code, 4)
+        if whence == 5:
+            send_stale(place, k)
+            return
+        landed(patch_from(place, whence), k)
+        for copy in passed(place, whence, k):
             copy.start()
 
-    def serve(which, k):
-        landed((slot_in(3), slot_in(1), slot_far(3), slot_far(1))[which], k)
-        condition, copy = forward(which, k)
-        pl.when(condition)(copy.start)
-
-    def when(condition, action, *arguments):
-        @pl.when(condition)
-        def _():
-            action(*arguments)
-
-    def late_one(k):
-        when(zh == 1, serve_z, k)
-        when(x > 0, serve, 0, k)
-        when(x == 3, serve, 1, k)
-
-    def late_two(k):
-        when(zh == 1, serve, 2, k)
-        when(zh == 1, serve, 3, k)
+    def steps(index):
+        for place in range(8):
+            if PLAN[place][index]:
+                @pl.when(pipe == place)
+                def _():
+                    for code in PLAN[place][index]:
+                        step(place, code)
+
+    def attend_next(index):
+        steps(3 + index)
+        slot = 0
+        for place in range(8):
+            patch = ATTEND[place][index]
+            slot = slot + jnp.where(pipe == place, patch, 0)
+            rest = [k for k in range(4) if patch != place and not awaited(place, patch, k)]
+            if rest:
+                @pl.when(pipe == place)
+                def _():
+                    for k in rest:
+                        landed(patch, k)
+        attend_slot(slot, index == 0)
 
     def project(k):
         rows = modbuf[k]
         for j in (1, 2):
             kv[pipe, k, j - 1] = jnp.dot(rows, wqkv[j], preferred_element_type=F32).astype(BF16)
-        send_own(k, True)
+        send_own(k)
         block = jnp.dot(rows, wqkv[0], preferred_element_type=F32).astype(BF16)
         for h in range(heads):
             q[h, k * 128 : (k + 1) * 128, :] = block[:, h * HEAD : (h + 1) * HEAD]
 
-    def early_far(k):
-        when(zh == 0, serve_z, k)
+    def late_in(k):
+        when(x > 0, serve, 0, k)
+        when(x == 3, serve, 1, k)
+
+    def late_far(k):
+        when(upper, serve, 4, k)
+
+    def late_far_two(k):
+        when(upper, serve, 2, k)
+        when(upper, serve, 3, k)
 
     def early_in(k):
         when(x == 0, serve, 0, k)
         when(x < 3, serve, 1, k)
+
+    def early_far(k):
+        when(zh == 0, serve, 4, k)
 
     def early_far_two(k):
         when(zh == 0, serve, 2, k)
@@ -208,78 +252,6 @@
             mod_out[direction][order].wait_recv()
             if order == 0:
                 mod_forward(direction).start()
-
-    for copy in stale_out:
-        copy.wait_send()
-    for order in range(2):
-        for direction in range(2):
-            mod_out[direction][order].start()
-
-    loads[3].wait()
-    project(0)
-
-    loads[4].wait()
-    for d in (1, 3, 2):
-        c = (seq + d) % 4
-        remote(sbuf.at[c], sbuf.at[c], st_s.at[0], st_r.at[c], at_seq(1)).wait_recv()
-    for k in range(4):
-        send_own(k, False)
-
-    loads[2].wait()
-    prb[seq] = normalized(prm[...].astype(F32)).astype(BF16)
-
-    late_one(0)
-    early_far(0)
-    mod_arrived(0)
-    project(1)
-    late_two(0)
-    early_far(1)
-    early_in(0)
-    early_in(1)
-
-    mod_arrived(1)
-    prompt_out = [
-        remote(prb.at[seq], prb.at[seq], pr_s.at[d - 1], pr_r.at[seq], at_seq(d)) for d in (1, 3, 2)
-    ]
-    for copy in prompt_out:
-        copy.start()
-    project(2)
-
-    loads[6].wait()
-    wout_out = [
-        remote(wout.at[seq], wout.at[seq], w_s.at[a], w_r.at[a], at_seq(1 if a == 0 else 3)) for a in range(2)
-    ]
-    for copy in wout_out:
-        copy.start()
-
-    late_one(1)
-    early_far(2)
-    early_far(3)
-    early_in(2)
-    early_in(3)
-    early_far_two(0)
-    early_far_two(1)
-    for direction in range(2):
-        mod_forward(direction).wait_recv()
-    project(3)
-    late_two(1)
-    late_one(2)
-
-    loads[5].wait()
-    for d in (1, 3, 2):
-        c = (seq + d) % 4
-        remote(prb.at[c], prb.at[c], pr_s.at[0], pr_r.at[c], at_seq(1)).wait_recv()
-    prompt_rows = prb[...].reshape(64, model)
-    for j in range(2):
-        pkv[x, j] = jnp.dot(prompt_rows, wpr[j], preferred_element_type=F32).astype(BF16)
-    pkv_out = [remote(pkv.at[x], pkv.at[x], pk_s.at[d - 1], pk_r.at[x], at_x(d)) for d in (1, 3, 2)]
-    for copy in pkv_out:
-        copy.start()
-
-    early_far_two(2)
-    early_far_two(3)
-    late_two(2)
-    late_one(3)
 
     def attend(keys_of, values_of, first):
         def one_head(h, carry):
@@ -312,19 +284,57 @@
             first,
         )
 
-    attend_slot(pipe, True)
-    late_two(3)
-    for d in (1, 3, 2):
-        c = (x + d) % 4
-        remote(pkv.at[c], pkv.at[c], pk_s.at[0], pk_r.at[c], at_x(1)).wait_recv()
-    attend(
-        lambda lanes: pkv[:, 0, :, lanes].reshape(256, HEAD),
-        lambda lanes: pkv[:, 1, :, lanes].reshape(256, HEAD),
-        False,
-    )
-    attend_slot(slot_in(3))
-    attend_slot(slot_in(1))
-    attend_slot(slot_far(0))
+    def stale_arrived():
+        loads[4].wait()
+        for d in (1, 3, 2):
+            c = (seq + d) % 4
+            remote(sbuf.at[c], sbuf.at[c], st_s.at[0], st_r.at[c], at_seq(1)).wait_recv()
+
+    def start_mod():
+        for copy in stale_out:
+            copy.wait_send()
+        for order in range(2):
+            for direction in range(2):
+                mod_out[direction][order].start()
+
+    prompt_out = [
+        remote(prb.at[seq], prb.at[seq], pr_s.at[d - 1], pr_r.at[seq], at_seq(d)) for d in (1, 3, 2)
+    ]
+    pkv_out = [remote(pkv.at[x], pkv.at[x], pk_s.at[d - 1], pk_r.at[x], at_x(d)) for d in (1, 3, 2)]
+
+    def prompt_rows():
+        loads[2].wait()
+        prb[seq] = normalized(prm[...].astype(F32)).astype(BF16)
+
+    def prompt_send():
+        for copy in prompt_out:
+            copy.start()
+
+    def prompt_project():
+        loads[5].wait()
+        for d in (1, 3, 2):
+            c = (seq + d) % 4
+            remote(prb.at[c], prb.at[c], pr_s.at[0], pr_r.at[c], at_seq(1)).wait_recv()
+        rows = prb[...].reshape(64, model)
+        for j in range(2):
+            pkv[x, j] = jnp.dot(rows, wpr[j], preferred_element_type=F32).astype(BF16)
+        for copy in pkv_out:
+            copy.start()
+
+    def prompt_attend():
+        for d in (1, 3, 2):
+            c = (x + d) % 4
+            remote(pkv.at[c], pkv.at[c], pk_s.at[0], pk_r.at[c], at_x(1)).wait_recv()
+        attend(
+            lambda lanes: pkv[:, 0, :, lanes].reshape(256, HEAD),
+            lambda lanes: pkv[:, 1, :, lanes].reshape(256, HEAD),
+            False,
+        )
+
+    def wout_copy(direction):
+        return remote(
+            wout.at[seq], wout.at[seq], w_s.at[direction], w_r.at[direction], at_seq(1 if direction == 0 else 3)
+        )
 
     def wout_arrival(direction):
         part = wout.at[(seq + (3 if direction == 0 else 1)) % 4]
@@ -334,21 +344,47 @@
         part = wout.at[source, pl.ds(direction * (width // 2), width // 2)]
         return remote(part, part, wf_s.at[direction], wf_r.at[direction], at_seq(1 if direction == 0 else 3))
 
-    wout_pass = []
-    for direction in range(2):
-        wout_arrival(direction).wait_recv()
-        copy = wout_forward(direction, (seq + (3 if direction == 0 else 1)) % 4)
-        copy.start()
-        wout_pass.append(copy)
-
-    attend_slot(slot_far(3))
-    attend_slot(slot_far(1))
-    for k in range(4):
-        landed(slot_in(2), k)
-    attend_slot(slot_in(2))
-    for k in range(4):
-        landed(slot_far(2), k)
-    attend_slot(slot_far(2))
+    wout_out = [wout_copy(direction) for direction in range(2)]
+    wout_pass = [wout_forward(direction, (seq + (3 if direction == 0 else 1)) % 4) for direction in range(2)]
+
+    def wout_send():
+        loads[6].wait()
+        for copy in wout_out:
+            copy.start()
+
+    def wout_serve():
+        for direction in range(2):
+            wout_arrival(direction).wait_recv()
+            wout_pass[direction].start()
+
+    def mod_last():
+        for direction in range(2):
+            mod_forward(direction).wait_recv()
+
+    loads[3].wait()
+    project(0)
+    start_mod()
+    stale_arrived()
+    prompt_rows()
+    steps(0)
+    mod_arrived(0)
+    project(1)
+    steps(1)
+    mod_arrived(1)
+    project(2)
+    steps(2)
+    mod_last()
+    prompt_send()
+    project(3)
+    wout_send()
+    for index in range(8):
+        attend_next(index)
+        if index == 1:
+            prompt_project()
+        if index == 5:
+            prompt_attend()
+        if index == 6:
+            wout_serve()
 
     att_out = []
     for h in range(heads):
@@ -390,11 +426,13 @@
     for k in range(4):
         for lane in range(3):
             piece(sbuf.at[k], pipe, k, lane, at_x(1)).wait_send()
-        for copy in spread_far(k):
-            copy.wait_send()
-        for which in range(4):
-            condition, copy = forward(which, k)
-            pl.when(condition)(copy.wait_send)
+    for place in range(8):
+        @pl.when(pipe == place)
+        def _():
+            for k in range(4):
+                for whence in range(5):
+                    for copy in passed(place, whence, k):
+                        copy.wait_send()
 
 
 def local(
@@ -434,7 +472,7 @@
             pltpu.VMEM((4, 2, rows // 2, width), BF16),
             dma((7,)), dma((3,)), dma((4,)), dma((2, 2)), dma((2, 2)), dma((2,)), dma((2,)),
             dma((3,)), dma((4,)), dma((3,)), dma((4,)), dma((2,)), dma((2,)), dma((2,)), dma((2,)),
-            dma((9, 4)), dma((8, 4)), dma((heads,)), dma((heads,)), dma((3, 2)), dma((4, 2)),
+            dma((18, 4)), dma((8, 4)), dma((heads,)), dma((heads,)), dma((3, 2)), dma((4, 2)),
         ],
         compiler_params=pltpu.CompilerParams(
             collective_id=0, has_side_effects=True, vmem_limit_bytes=58 * 2**20

time: 121 us -> 102 us (0.84)
  the two profiles are of different devices: /device:TPU:75 before, /device:TPU:88 now
where the time goes in v3:
time: 102 us
  Pallas kernels  99.2 us (97%)
  local copies, waits for them, and re-layouts  1.77 us (2%)
  between operations  1.31 us (1%)
    pallas_call x1, Pallas kernels, local(): pl.pallas_call(kernel, out_shape=jax.ShapeDtypeStruct((rows, half), BF16)...  99.2 us

profile of v3, /device:TPU:88, one launch (start us, length us, event | category | flops | bytes accessed | tf_op | source)
XLA Modules:
  0.0 102.2 jit_solution(9954257445661480881)
XLA Ops:
  1.3 99.2 %guided_attention.1 = bf16[128,1536]{1,0:T(8,128)(2,1)} custom-call(bf16[1,128,3072]{2,1,0:T(8,128)(2,1)} %img_in.1, bf16[1,64,3072]{2,1,0:T(8,128)(2,1)} %prm_in.1, bf16[1,2,128,1536]{3,2,1,0:T(8,128)(2,1)} %stale_in.1, bf16[3,3072,384]{2,1,0:T(8,128)(2,1)} %wqkv_in.1, bf16[2,3072,384]{2,1,0:T(8,128)(2,1)} %wpr_in.1, bf16[384,3072]{1,0:T(8,128)(2,1)} %wout_in.1, ...), custom_call_target="tpu_custom_call" | custom-call | tf_op jit(solution)/shard_map/guided_attention/pallas_call | solution.py:449
  100.5 1.8 %copy.13 = bf16[128,1536]{1,0:T(8,128)(2,1)} copy(bf16[128,1536]{1,0:T(8,128)(2,1)} %guided_attention.1) | data formatting | bytes 786432

commit v4 on v3

--- a/solution.py
+++ b/solution.py
@@ -14,38 +14,38 @@
 
 
 PLAN = (
-    ((20, 21, 22, 23, 16), (17, 18), (19, 12), (13,), (3,), (14,), (15,), (), (1,), (), ()),
-    ((20, 21, 22, 23, 0, 16, 4), (17, 5, 18, 6, 1), (19, 7), (), (2,), (14,), (), (3,), (15,), (), ()),
-    ((20, 21, 22, 23, 0, 16, 4), (17, 18, 6), (1, 12, 13), (14,), (), (2, 15), (), (19,), (3,), (), ()),
-    ((20, 21, 22, 23, 0, 16), (17, 12, 8, 5), (1, 19, 13, 9, 14), (), (2, 15), (3,), (7,), (18,), (), (), ()),
-    ((20, 21, 22, 23, 16, 4), (5, 1, 17, 6), (7, 3, 12, 8, 18), (), (), (), (9, 19), (10, 13, 11), (), (), ()),
-    ((20, 21, 22, 23, 16, 0, 4), (8, 5, 6), (9, 17, 2, 18), (), (), (19,), (7, 10), (), (11,), (), ()),
-    ((20, 21, 22, 16, 0, 4), (5, 17, 1, 6), (7, 23, 18, 2), (), (), (19,), (3,), (10,), (11,), (), ()),
-    ((20, 21, 22, 23, 16), (8, 17, 5), (18,), (9,), (19,), (), (10, 7), (), (), (11,), ()),
+    ((17,), (14, 1, 16, 8), (12, 10), (9,), (15, 11), (18, 19), (3,), (), (13,), (), ()),
+    ((20, 16, 5, 0), (18, 6, 14, 1), (19, 4, 15), (), (21, 2, 17), (22, 23, 3), (7,), (), (), (), ()),
+    ((21, 22, 16, 4, 20, 0, 18), (17, 1), (14, 12), (19, 2), (23,), (6, 3), (13,), (15,), (), (), ()),
+    ((20, 21, 16), (0, 8, 13, 18), (17, 1, 12, 19), (), (22,), (23, 9, 2, 3), (14,), (15,), (), (), ()),
+    ((21, 16, 20, 6), (4, 17, 7), (9, 18, 13), (), (22, 8, 23, 19), (5,), (11,), (10,), (12,), (), ()),
+    ((20, 22, 0, 6, 23, 8, 7), (17, 5, 9), (21, 2, 18, 16, 19), (), (4,), (10,), (), (11,), (), (), ()),
+    ((20, 22, 0, 23, 21, 6), (4, 7, 17, 1), (18, 2), (), (16, 5), (19,), (3,), (10,), (), (11,), ()),
+    ((20, 21, 22, 23, 16), (17, 8, 13), (18, 12, 9, 5, 14), (), (19,), (7,), (10,), (15,), (11,), (), ()),
 )
 ATTEND = (
-    (0, 4, 1, 5, 2, 3, 6, 7),
-    (1, 5, 2, 4, 0, 6, 7, 3),
-    (2, 3, 7, 5, 6, 1, 4, 0),
-    (3, 4, 2, 0, 7, 6, 1, 5),
-    (4, 5, 7, 0, 3, 1, 6, 2),
-    (5, 7, 1, 6, 4, 0, 2, 3),
-    (6, 7, 2, 5, 3, 1, 4, 0),
-    (7, 3, 6, 4, 0, 5, 2, 1),
+    (0, 7, 4, 3, 1, 5, 6, 2),
+    (1, 5, 0, 2, 6, 4, 3, 7),
+    (2, 6, 1, 3, 7, 5, 4, 0),
+    (3, 7, 2, 6, 4, 0, 5, 1),
+    (4, 0, 5, 7, 3, 1, 2, 6),
+    (5, 1, 4, 6, 0, 7, 3, 2),
+    (6, 7, 2, 5, 3, 4, 1, 0),
+    (7, 3, 4, 6, 0, 5, 2, 1),
 )
-
+EARLY = (0, 1, 3, 2, 2, 4, 4, 4)
 
 def passes_to(place, whence, k):
     upper, x = divmod(place, 4)
     if not upper:
         x = 3 - x
         whence = (1, 0, 3, 2, 4)[whence]
-    far = k in (2, 3)
+    far, near = k in (2, 3), k in (0, 1, 2, 3)
     ways = {
-        0: "+" if x == 2 or (x == 1 and k % 2 == 0) or (x == 0 and k % 2 == 1) else "",
-        1: ("-" if x == 1 or (x == 2 and k % 2 == 0) or (x == 3 and k % 2 == 1) else "") + ("z" if x < 3 else ""),
+        0: "+" if x == 2 or (x == 1 and k % 2 == 0) or (x == 0 and not near) else "",
+        1: ("-" if x == 1 or (x == 2 and near) or (x == 3 and k % 2 == 1) else "") + ("z" if x < 3 else ""),
         2: "+" if x != 2 or far else "",
-        3: "-" if x == 0 and not far else "",
+        3: ("-" if x == 0 and not far else "") + ("z" if x == 3 else ""),
         4: "+-" if x == 3 else "-",
     }[whence]
     return ways if upper else ways.translate(str.maketrans("+-", "-+"))
@@ -71,7 +71,7 @@
     img_in, prm_in, stale_in, wqkv_in, wpr_in, wout_in, table_in, step_in, guide_in,
     out_ref,
     img, table, prm, wqkv, wpr, wout, modbuf, prb, pkv, sbuf, kv, q, acc, top, att, peer, mix, mixall,
-    lsem, st_s, st_r, m_s, m_r, mf_s, mf_r, pr_s, pr_r, pk_s, pk_r, w_s, w_r, wf_s, wf_r, ss, rs,
+    lsem, st_s, st_r, m_s, m_r, mf_s, mf_r, pr_s, pr_r, pk_s, pk_r, w_s, w_r, wf_s, wf_r, ss, rs, v_s, v_r, u_s, u_r,
     a_s, a_r, x_s, x_r,
 ):
     dp, cfg, pipe, seq = (lax.axis_index(name) for name in ("dp", "cfg", "pipe", "seq"))
@@ -89,6 +89,9 @@
 
     at_z = (dp, cfg, (1 - zh) * 4 + x, seq)
     at_core = (dp, 1 - cfg, pipe, seq)
+    line = zh * 2 + dp
+    at_line = [(1 - dp, cfg, pipe, seq), at_z, (1 - dp, cfg, (1 - zh) * 4 + x, seq)]
+    line_of = [zh * 2 + 1 - dp, (1 - zh) * 2 + dp, (1 - zh) * 2 + 1 - dp]
 
     def remote(src, dst, s, r, device):
         return pltpu.make_async_remote_copy(
@@ -96,7 +99,7 @@
         )
 
     barrier = pltpu.get_barrier_semaphore()
-    partners = [at_seq(1), at_seq(3), at_seq(2), at_x(1), at_x(3), at_x(2), at_z, at_core]
+    partners = [at_seq(1), at_seq(3), at_seq(2), at_x(1), at_x(3), at_x(2), at_core] + at_line
     for device in partners:
         pl.semaphore_signal(barrier, inc=1, device_id=device, device_id_type=MESH)
 
@@ -104,15 +107,23 @@
 
     def seq_cols(d):
         return pl.ds(pl.multiple_of((seq + d) % 4 * width, 128), width)
+
+    def stale_part(k, source):
+        return sbuf.at[k, :, pl.ds(pl.multiple_of(source * 32, 32), 32)]
 
     loads = [
         pltpu.make_async_copy(img_in.at[0], img, lsem.at[0]),
         pltpu.make_async_copy(table_in, table, lsem.at[1]),
         pltpu.make_async_copy(prm_in.at[0, pl.ds(pl.multiple_of(x * 16, 16), 16)], prm, lsem.at[2]),
         pltpu.make_async_copy(wqkv_in, wqkv, lsem.at[3]),
-        pltpu.make_async_copy(stale_in.at[0, :, :, seq_cols(0)], sbuf.at[seq], lsem.at[4]),
+        pltpu.make_async_copy(stale_in.at[0, :, pl.ds(0, 32), seq_cols(0)], stale_part(0, seq), lsem.at[4]),
         pltpu.make_async_copy(wpr_in, wpr, lsem.at[5]),
         pltpu.make_async_copy(wout_in.at[:, half_cols], wout.at[seq], lsem.at[6]),
+    ] + [
+        pltpu.make_async_copy(
+            stale_in.at[0, :, pl.ds(k * 32, 32), seq_cols(0)], stale_part(k, seq), lsem.at[6 + k]
+        )
+        for k in (1, 2, 3)
     ]
     for load in loads:
         load.start()
@@ -134,12 +145,31 @@
     modulate(0, 64)
     pl.semaphore_wait(barrier, len(partners))
 
-    stale_out = [
-        remote(stale_in.at[0, :, :, seq_cols(d)], sbuf.at[seq], st_s.at[d - 1], st_r.at[seq], at_seq(d))
-        for d in (2, 1, 3)
-    ]
-    for copy in stale_out:
-        copy.start()
+    def any_of(places):
+        found = pipe == places[0]
+        for place in places[1:]:
+            found = found | (pipe == place)
+        return found
+
+    def stale_copy(k, d, source):
+        return remote(
+            stale_in.at[0, :, pl.ds(k * 32, 32), seq_cols(d)], stale_part(k, source),
+            st_s.at[d - 1, k], st_r.at[source, k], at_seq(d),
+        )
+
+    stale_out = [[stale_copy(k, d, seq) for d in (2, 1, 3)] for k in range(4)]
+    early = [[place for place in range(1, 8) if EARLY[place] > k] for k in range(4)]
+    late = [[place for place in range(1, 8) if EARLY[place] <= k] for k in range(4)]
+
+    def each_stale(places, act):
+        for k in range(4):
+            if places[k]:
+                @pl.when(any_of(places[k]))
+                def _():
+                    for copy in stale_out[k]:
+                        act(copy)
+
+    each_stale(early, lambda copy: copy.start())
     modulate(64, 64)
 
     def half_rows(half):
@@ -163,16 +193,25 @@
     def piece(source, slot, k, lane, device):
         return remote(source, kv.at[slot, k], ss.at[lane, k], rs.at[slot, k], device)
 
+    att_out = [remote(att.at[h], peer.at[h], a_s.at[h], a_r.at[h], at_core) for h in range(heads)]
+
+    def send_attended(h):
+        block = acc[h]
+        att[h] = block[:, :HEAD] / block[:, HEAD : HEAD + 1]
+        att_out[h].start()
+
     def toward(way):
         return {"+": at_x(1), "-": at_x(3), "z": at_z}[way]
 
     def send_own(k):
-        for condition, lane, way in ((x < 3, 0, "+"), (x == 0, 1, "-"), (zh == 0, 2, "z")):
+        for condition, lane, way in ((x < 3, 0, "+"), (pipe == 4, 1, "-"), (zh == 0, 2, "z")):
             pl.when(condition)(piece(kv.at[pipe, k], pipe, k, lane, toward(way)).start)
 
     def send_stale(place, k):
         upper, column = divmod(place, 4)
-        ways = (("+", 0),) * (column == 3) + (("-", 1),) * (column > 0) + (("z", 2),) * upper
+        for d in (1, 3, 2):
+            stale_copy(k, d, (seq + d) % 4).wait_recv()
+        ways = (("+", 0),) * (place == 3) + (("-", 1),) * (column > 0) + (("z", 2),) * upper
         for way, lane in ways:
             piece(sbuf.at[k], place, k, lane, toward(way)).start()
 
@@ -214,7 +253,7 @@
                 def _():
                     for k in rest:
                         landed(patch, k)
-        attend_slot(slot, index == 0)
+        attend_slot(slot, index == 0, send_attended if index == 7 else None)
 
     def project(k):
         rows = modbuf[k]
@@ -253,46 +292,40 @@
             if order == 0:
                 mod_forward(direction).start()
 
-    def attend(keys_of, values_of, first):
-        def one_head(h, carry):
-            lanes = pl.ds(pl.multiple_of(h * HEAD, HEAD), HEAD)
-            keys = keys_of(lanes)
-            values = values_of(lanes)
-            values = jnp.concatenate([values, jnp.ones_like(values)], axis=1)
-            scores = lax.dot_general(q[h], keys, (((1,), (1,)), ((), ())), preferred_element_type=F32)
-            peak = jnp.max(scores, axis=1, keepdims=True)
-            if first:
-                new_top = peak
-            else:
-                old_top = top[h][:, :1]
-                new_top = jnp.maximum(old_top, peak)
-            weights = jnp.exp2(scores * scale - new_top * scale).astype(BF16)
-            part = jnp.dot(weights, values, preferred_element_type=F32)
-            if first:
-                acc[h] = part
-            else:
-                acc[h] = acc[h] * jnp.exp2((old_top - new_top) * scale) + part
-            top[h] = jnp.broadcast_to(new_top, top.shape[1:])
-            return carry
-
-        lax.fori_loop(0, heads, one_head, 0)
-
-    def attend_slot(slot, first=False):
+    def attend_head(h, keys, values, first):
+        values = jnp.concatenate([values, jnp.ones_like(values)], axis=1)
+        scores = lax.dot_general(q[h], keys, (((1,), (1,)), ((), ())), preferred_element_type=F32)
+        peak = jnp.max(scores, axis=1, keepdims=True)
+        if first:
+            new_top = peak
+        else:
+            old_top = top[h][:, :1]
+            new_top = jnp.maximum(old_top, peak)
+        weights = jnp.exp2(scores * scale - new_top * scale).astype(BF16)
+        part = jnp.dot(weights, values, preferred_element_type=F32)
+        if first:
+            acc[h] = part
+        else:
+            acc[h] = acc[h] * jnp.exp2((old_top - new_top) * scale) + part
+        top[h] = jnp.broadcast_to(new_top, top.shape[1:])
+
+    def attend(keys_of, values_of, first, finish=None):
+        for h in range(heads):
+            lanes = pl.ds(h * HEAD, HEAD)
+            attend_head(h, keys_of(lanes), values_of(lanes), first)
+            if finish is not None:
+                finish(h)
+
+
+    def attend_slot(slot, first=False, finish=None):
         attend(
             lambda lanes: kv[slot, :, 0, :, lanes].reshape(512, HEAD),
             lambda lanes: kv[slot, :, 1, :, lanes].reshape(512, HEAD),
             first,
+            finish,
         )
 
-    def stale_arrived():
-        loads[4].wait()
-        for d in (1, 3, 2):
-            c = (seq + d) % 4
-            remote(sbuf.at[c], sbuf.at[c], st_s.at[0], st_r.at[c], at_seq(1)).wait_recv()
-
     def start_mod():
-        for copy in stale_out:
-            copy.wait_send()
         for order in range(2):
             for direction in range(2):
                 mod_out[direction][order].start()
@@ -331,43 +364,80 @@
             False,
         )
 
+    share = out_half // 3
+    quarter = width // 4
+
     def wout_copy(direction):
-        return remote(
-            wout.at[seq], wout.at[seq], w_s.at[direction], w_r.at[direction], at_seq(1 if direction == 0 else 3)
-        )
+        part = wout.at[seq, :, pl.ds(0, out_half - share)]
+        return remote(part, part, w_s.at[direction], w_r.at[direction], at_seq(1 if direction == 0 else 3))
 
     def wout_arrival(direction):
-        part = wout.at[(seq + (3 if direction == 0 else 1)) % 4]
+        part = wout.at[(seq + (3 if direction == 0 else 1)) % 4, :, pl.ds(0, out_half - share)]
         return remote(part, part, w_s.at[direction], w_r.at[direction], at_seq(1))
 
     def wout_forward(direction, source):
-        part = wout.at[source, pl.ds(direction * (width // 2), width // 2)]
+        part = wout.at[source, pl.ds(direction * (width // 2), width // 2), pl.ds(0, out_half - share)]
         return remote(part, part, wf_s.at[direction], wf_r.at[direction], at_seq(1 if direction == 0 else 3))
+
+    def wout_quarter(source, place):
+        rows = pl.ds(pl.multiple_of(place * quarter, 16), quarter)
+        return wout.at[source, rows, pl.ds(out_half - share, share)]
+
+    def quarter_copy(source, d):
+        part = wout_quarter(source, line)
+        return remote(part, part, v_s.at[d - 1], v_r.at[source], at_seq(d))
+
+    def quarter_pass(d, to):
+        source = (seq + d) % 4
+        part = wout_quarter(source, line)
+        return remote(part, part, u_s.at[d - 1, to], u_r.at[source, line], at_line[to])
+
+    def quarter_arrival(d, place):
+        source = (seq + d) % 4
+        part = wout_quarter(source, place)
+        return remote(part, part, u_s.at[0, 0], u_r.at[source, place], at_line[0])
 
     wout_out = [wout_copy(direction) for direction in range(2)]
     wout_pass = [wout_forward(direction, (seq + (3 if direction == 0 else 1)) % 4) for direction in range(2)]
+    quarter_out = [quarter_copy(seq, d) for d in (2, 1, 3)]
+    quarter_on = [[quarter_pass(d, to) for to in range(3)] for d in (1, 3, 2)]
 
     def wout_send():
         loads[6].wait()
-        for copy in wout_out:
+        for copy in quarter_out + wout_out:
             copy.start()
+
+    def quarter_serve():
+        for d, copies in zip((1, 3, 2), quarter_on):
+            quarter_copy((seq + d) % 4, 1).wait_recv()
+            for copy in copies:
+                copy.start()
 
     def wout_serve():
         for direction in range(2):
             wout_arrival(direction).wait_recv()
             wout_pass[direction].start()
 
+    def wout_last():
+        for direction in range(2):
+            wout_forward(direction, (seq + 2) % 4).wait_recv()
+        for d in (1, 3, 2):
+            for place in line_of:
+                quarter_arrival(d, place).wait_recv()
+
     def mod_last():
         for direction in range(2):
             mod_forward(direction).wait_recv()
 
+    start_mod()
     loads[3].wait()
     project(0)
-    start_mod()
-    stale_arrived()
+    for load in [loads[4]] + loads[7:]:
+        load.wait()
     prompt_rows()
     steps(0)
     mod_arrived(0)
+    each_stale(late, lambda copy: copy.start())
     project(1)
     steps(1)
     mod_arrived(1)
@@ -382,50 +452,51 @@
         if index == 1:
             prompt_project()
         if index == 5:
+            quarter_serve()
             prompt_attend()
         if index == 6:
             wout_serve()
 
-    att_out = []
-    for h in range(heads):
-        block = acc[h]
-        att[h] = block[:, :HEAD] / block[:, HEAD : HEAD + 1]
-        copy = remote(att.at[h], peer.at[h], a_s.at[h], a_r.at[h], at_core)
-        copy.start()
-        att_out.append(copy)
     guide = guide_in[0]
     first_side = cfg == 0
+    mix_out = []
     for h in range(heads):
+        lanes = pl.ds(h * HEAD, HEAD)
         att_out[h].wait_recv()
         mine, other = att[h], peer[h]
         cond_part = jnp.where(first_side, mine, other)
         uncond = jnp.where(first_side, other, mine)
         mixed = (uncond + guide * (cond_part - uncond)).astype(BF16)
-        mix[:, :, :, h * HEAD : (h + 1) * HEAD] = mixed.reshape(4, 2, 64, HEAD)
-    mix_out = [
-        remote(mix.at[group, part], mixall.at[seq, half], x_s.at[d - 1, half], x_r.at[seq, half], at_seq(d))
-        for d, half, group, part in ((2, 0, 3, 0), (2, 1, 3, 1), (1, 0, 2, 1), (1, 1, 1, 1), (3, 0, 1, 0), (3, 1, 2, 0))
-    ]
-    for copy in mix_out:
-        copy.start()
+        mix[:, :, :, lanes] = mixed.reshape(4, 2, 64, HEAD)
+        for d, half, group, part in (
+            (2, 0, 3, 0), (2, 1, 3, 1), (1, 0, 2, 1), (1, 1, 1, 1), (3, 0, 1, 0), (3, 1, 2, 0),
+        ):
+            copy = remote(
+                mix.at[group, part, :, lanes], mixall.at[seq, half, :, lanes],
+                x_s.at[h, d - 1, half], x_r.at[h, seq, half], at_seq(d),
+            )
+            copy.start()
+            mix_out.append(copy)
     total = jnp.dot(mix[0].reshape(128, width), wout[seq], preferred_element_type=F32)
-    for direction in range(2):
-        wout_forward(direction, (seq + 2) % 4).wait_recv()
+    wout_last()
     for d in (1, 3, 2):
         c = (seq + d) % 4
-        for half in range(2):
-            here = mixall.at[c, half]
-            remote(here, here, x_s.at[0, 0], x_r.at[c, half], at_seq(1)).wait_recv()
+        for h in range(heads):
+            for half in range(2):
+                here = mixall.at[c, half, :, pl.ds(h * HEAD, HEAD)]
+                remote(here, here, x_s.at[0, 0, 0], x_r.at[h, c, half], at_seq(1)).wait_recv()
         total = total + jnp.dot(mixall[c].reshape(128, width), wout[c], preferred_element_type=F32)
     out_ref[...] = (table[2, pl.ds(now, 1), half_cols] * total).astype(BF16)
 
-    for copy in mod_out[0] + mod_out[1] + prompt_out + pkv_out + wout_out + wout_pass + att_out + mix_out:
+    for copy in sum(quarter_on, quarter_out) + mod_out[0] + mod_out[1] + prompt_out + pkv_out + wout_out + wout_pass + att_out + mix_out:
         copy.wait_send()
     for direction in range(2):
         mod_forward(direction).wait_send()
+    each_stale(early, lambda copy: copy.wait_send())
+    each_stale(late, lambda copy: copy.wait_send())
     for k in range(4):
-        for lane in range(3):
-            piece(sbuf.at[k], pipe, k, lane, at_x(1)).wait_send()
+        for condition, lane in ((pipe != 7, 0), (pipe != 0, 1), (pipe >= 0, 2)):
+            pl.when(condition)(piece(sbuf.at[k], pipe, k, lane, at_x(1)).wait_send)
     for place in range(8):
         @pl.when(pipe == place)
         def _():
@@ -470,9 +541,9 @@
             pltpu.VMEM((heads, 4 * rows, HEAD), F32),
             pltpu.VMEM((4, 2, rows // 2, width), BF16),
             pltpu.VMEM((4, 2, rows // 2, width), BF16),
-            dma((7,)), dma((3,)), dma((4,)), dma((2, 2)), dma((2, 2)), dma((2,)), dma((2,)),
+            dma((10,)), dma((3, 4)), dma((4, 4)), dma((2, 2)), dma((2, 2)), dma((2,)), dma((2,)),
             dma((3,)), dma((4,)), dma((3,)), dma((4,)), dma((2,)), dma((2,)), dma((2,)), dma((2,)),
-            dma((18, 4)), dma((8, 4)), dma((heads,)), dma((heads,)), dma((3, 2)), dma((4, 2)),
+            dma((18, 4)), dma((8, 4)), dma((3,)), dma((4,)), dma((3, 3)), dma((4, 4)), dma((heads,)), dma((heads,)), dma((heads, 3, 2)), dma((heads, 4, 2)),
         ],
         compiler_params=pltpu.CompilerParams(
             collective_id=0, has_side_effects=True, vmem_limit_bytes=58 * 2**20

time: 102 us -> 93.5 us (0.917)
  the two profiles are of different devices: /device:TPU:88 before, /device:TPU:6 now
where the time goes in v4:
time: 93.5 us; the launch traced here: 93.3 us
  Pallas kernels  90.2 us (96%)
  local copies, waits for them, and re-layouts  1.77 us (2%)
  between operations  1.31 us (1%)
    pallas_call x1, Pallas kernels, local(): pl.pallas_call(kernel, out_shape=jax.ShapeDtypeStruct((rows, half), BF16)...  90.2 us

profile of v4, /device:TPU:6, one launch (start us, length us, event | category | flops | bytes accessed | tf_op | source)
XLA Modules:
  0.0 93.3 jit_solution(16736133466822926737)
XLA Ops:
  1.3 90.2 %guided_attention.1 = bf16[128,1536]{1,0:T(8,128)(2,1)} custom-call(bf16[1,128,3072]{2,1,0:T(8,128)(2,1)} %img_in.1, bf16[1,64,3072]{2,1,0:T(8,128)(2,1)} %prm_in.1, bf16[1,2,128,1536]{3,2,1,0:T(8,128)(2,1)} %stale_in.1, bf16[3,3072,384]{2,1,0:T(8,128)(2,1)} %wqkv_in.1, bf16[2,3072,384]{2,1,0:T(8,128)(2,1)} %wpr_in.1, bf16[384,3072]{1,0:T(8,128)(2,1)} %wout_in.1, ...), custom_call_target="tpu_custom_call" | custom-call | tf_op jit(solution)/shard_map/guided_attention/pallas_call | solution.py:520
  91.5 1.8 %copy.13 = bf16[128,1536]{1,0:T(8,128)(2,1)} copy(bf16[128,1536]{1,0:T(8,128)(2,1)} %guided_attention.1) | data formatting | bytes 786432

commit v5 on v4

--- a/solution.py
+++ b/solution.py
@@ -14,26 +14,26 @@
 
 
 PLAN = (
-    ((17,), (14, 1, 16, 8), (12, 10), (9,), (15, 11), (18, 19), (3,), (), (13,), (), ()),
-    ((20, 16, 5, 0), (18, 6, 14, 1), (19, 4, 15), (), (21, 2, 17), (22, 23, 3), (7,), (), (), (), ()),
-    ((21, 22, 16, 4, 20, 0, 18), (17, 1), (14, 12), (19, 2), (23,), (6, 3), (13,), (15,), (), (), ()),
-    ((20, 21, 16), (0, 8, 13, 18), (17, 1, 12, 19), (), (22,), (23, 9, 2, 3), (14,), (15,), (), (), ()),
-    ((21, 16, 20, 6), (4, 17, 7), (9, 18, 13), (), (22, 8, 23, 19), (5,), (11,), (10,), (12,), (), ()),
-    ((20, 22, 0, 6, 23, 8, 7), (17, 5, 9), (21, 2, 18, 16, 19), (), (4,), (10,), (), (11,), (), (), ()),
-    ((20, 22, 0, 23, 21, 6), (4, 7, 17, 1), (18, 2), (), (16, 5), (19,), (3,), (10,), (), (11,), ()),
-    ((20, 21, 22, 23, 16), (17, 8, 13), (18, 12, 9, 5, 14), (), (19,), (7,), (10,), (15,), (11,), (), ()),
+    ((), (8, 19), (17, 18), (), (16,), (11, 12, 10, 1, 14, 9), (13,), (3,), (15,), (), ()),
+    ((0, 20, 16), (1, 18, 4, 5), (14, 21, 2), (), (22, 23, 3, 17), (6,), (7, 19), (), (), (15,), ()),
+    ((0, 4, 20, 16, 21), (18, 1, 12), (13, 15), (), (22, 2, 17, 23, 14), (3,), (6, 19), (), (), (), ()),
+    ((20, 0, 16, 17), (8, 21, 1, 19, 18), (15, 13), (14,), (22, 2), (23, 12), (3,), (9,), (), (), ()),
+    ((21, 16, 23, 22, 17), (20, 4, 6, 8, 18), (9, 5, 19), (), (), (12, 10, 7), (11,), (13,), (), (), ()),
+    ((20, 0, 22, 5, 8, 6), (4, 16, 21), (9, 18), (), (23, 10), (17, 2, 19), (7,), (), (11,), (), ()),
+    ((20, 21, 0, 22, 16, 4, 5), (7, 1), (6, 2, 23), (17, 18), (), (19, 3), (), (10,), (11,), (), ()),
+    ((20, 21, 22, 23, 16), (8, 17, 13), (5, 9, 18), (12,), (14, 19), (15,), (), (10, 7), (), (11,), ()),
 )
 ATTEND = (
-    (0, 7, 4, 3, 1, 5, 6, 2),
-    (1, 5, 0, 2, 6, 4, 3, 7),
-    (2, 6, 1, 3, 7, 5, 4, 0),
-    (3, 7, 2, 6, 4, 0, 5, 1),
-    (4, 0, 5, 7, 3, 1, 2, 6),
-    (5, 1, 4, 6, 0, 7, 3, 2),
-    (6, 7, 2, 5, 3, 4, 1, 0),
-    (7, 3, 4, 6, 0, 5, 2, 1),
+    (0, 4, 7, 1, 3, 5, 2, 6),
+    (1, 0, 4, 2, 5, 7, 6, 3),
+    (2, 7, 1, 6, 0, 3, 4, 5),
+    (3, 7, 4, 2, 1, 0, 6, 5),
+    (4, 0, 5, 3, 7, 1, 6, 2),
+    (5, 7, 1, 6, 4, 0, 3, 2),
+    (6, 7, 2, 5, 3, 1, 4, 0),
+    (7, 3, 0, 6, 4, 5, 2, 1),
 )
-EARLY = (0, 1, 3, 2, 2, 4, 4, 4)
+EARLY = (0, 2, 2, 2, 4, 3, 4, 4)
 
 def passes_to(place, whence, k):
     upper, x = divmod(place, 4)

time: 93.5 us -> 92 us (0.984)
  Pallas kernels: 90.2 us -> 88.8 us
    pallas_call x1, Pallas kernels: 90.2 us -> 88.8 us  [local(): pl.pallas_call(kernel, out_shape=jax.ShapeDtypeStruct((rows, half), BF16)...]
where the time goes in v5:
time: 92 us; the launch traced here: 91.9 us
  Pallas kernels  88.8 us (97%)
  local copies, waits for them, and re-layouts  1.77 us (2%)
  between operations  1.31 us (1%)
    pallas_call x1, Pallas kernels, local(): pl.pallas_call(kernel, out_shape=jax.ShapeDtypeStruct((rows, half), BF16)...  88.8 us

profile of v5, /device:TPU:6, one launch (start us, length us, event | category | flops | bytes accessed | tf_op | source)
XLA Modules:
  0.0 91.9 jit_solution(8051462962470599433)
XLA Ops:
  1.3 88.8 %guided_attention.1 = bf16[128,1536]{1,0:T(8,128)(2,1)} custom-call(bf16[1,128,3072]{2,1,0:T(8,128)(2,1)} %img_in.1, bf16[1,64,3072]{2,1,0:T(8,128)(2,1)} %prm_in.1, bf16[1,2,128,1536]{3,2,1,0:T(8,128)(2,1)} %stale_in.1, bf16[3,3072,384]{2,1,0:T(8,128)(2,1)} %wqkv_in.1, bf16[2,3072,384]{2,1,0:T(8,128)(2,1)} %wpr_in.1, bf16[384,3072]{1,0:T(8,128)(2,1)} %wout_in.1, ...), custom_call_target="tpu_custom_call" | custom-call | tf_op jit(solution)/shard_map/guided_attention/pallas_call | solution.py:520
  90.1 1.8 %copy.13 = bf16[128,1536]{1,0:T(8,128)(2,1)} copy(bf16[128,1536]{1,0:T(8,128)(2,1)} %guided_attention.1) | data formatting | bytes 786432

commit v6 on v5

--- a/solution.py
+++ b/solution.py
@@ -14,26 +14,26 @@
 
 
 PLAN = (
-    ((), (8, 19), (17, 18), (), (16,), (11, 12, 10, 1, 14, 9), (13,), (3,), (15,), (), ()),
-    ((0, 20, 16), (1, 18, 4, 5), (14, 21, 2), (), (22, 23, 3, 17), (6,), (7, 19), (), (), (15,), ()),
-    ((0, 4, 20, 16, 21), (18, 1, 12), (13, 15), (), (22, 2, 17, 23, 14), (3,), (6, 19), (), (), (), ()),
-    ((20, 0, 16, 17), (8, 21, 1, 19, 18), (15, 13), (14,), (22, 2), (23, 12), (3,), (9,), (), (), ()),
-    ((21, 16, 23, 22, 17), (20, 4, 6, 8, 18), (9, 5, 19), (), (), (12, 10, 7), (11,), (13,), (), (), ()),
-    ((20, 0, 22, 5, 8, 6), (4, 16, 21), (9, 18), (), (23, 10), (17, 2, 19), (7,), (), (11,), (), ()),
-    ((20, 21, 0, 22, 16, 4, 5), (7, 1), (6, 2, 23), (17, 18), (), (19, 3), (), (10,), (11,), (), ()),
-    ((20, 21, 22, 23, 16), (8, 17, 13), (5, 9, 18), (12,), (14, 19), (15,), (), (10, 7), (), (11,), ()),
+    ((), (17, 1, 18), (9, 16), (12, 19), (), (8, 14, 10, 13, 11), (3,), (), (), (15,), ()),
+    ((20, 0, 4, 16, 5, 17), (1, 18, 21), (15, 14), (), (22, 2, 23, 3), (6, 19), (), (7,), (), (), ()),
+    ((20, 21, 0, 17, 4), (12, 6, 19), (1, 13), (15,), (22, 16, 2, 23, 18, 14, 3), (), (), (), (), (), ()),
+    ((21, 20, 22, 0, 17), (13, 9, 1, 16, 18), (19, 2, 14), (), (23, 12), (3, 15), (), (8,), (), (), ()),
+    ((21, 22, 4, 16, 20, 23, 17), (6, 5), (18, 9, 19), (8, 12), (), (10, 7), (13,), (11,), (), (), ()),
+    ((20, 21, 22, 0, 5), (8, 7, 6, 16), (9, 18), (), (23, 17, 4), (2, 19), (), (10,), (11,), (), ()),
+    ((21, 0, 4, 23, 22, 16, 5), (7, 20, 17, 1), (6, 18, 2), (), (), (19, 3), (), (10, 11), (), (), ()),
+    ((20, 21, 22, 23, 12, 8), (16, 13, 17), (9, 18), (), (10, 14, 5, 19, 15), (), (), (11, 7), (), (), ()),
 )
 ATTEND = (
-    (0, 4, 7, 1, 3, 5, 2, 6),
-    (1, 0, 4, 2, 5, 7, 6, 3),
-    (2, 7, 1, 6, 0, 3, 4, 5),
-    (3, 7, 4, 2, 1, 0, 6, 5),
-    (4, 0, 5, 3, 7, 1, 6, 2),
-    (5, 7, 1, 6, 4, 0, 3, 2),
-    (6, 7, 2, 5, 3, 1, 4, 0),
-    (7, 3, 0, 6, 4, 5, 2, 1),
+    (0, 4, 7, 3, 1, 6, 5, 2),
+    (1, 0, 5, 4, 2, 6, 3, 7),
+    (2, 6, 7, 1, 3, 0, 4, 5),
+    (3, 7, 2, 4, 6, 0, 1, 5),
+    (4, 0, 5, 7, 3, 6, 2, 1),
+    (5, 6, 1, 4, 7, 0, 2, 3),
+    (6, 7, 2, 5, 1, 3, 4, 0),
+    (7, 3, 6, 0, 5, 2, 4, 1),
 )
-EARLY = (0, 2, 2, 2, 4, 3, 4, 4)
+EARLY = (0, 2, 2, 3, 4, 3, 4, 4)
 
 def passes_to(place, whence, k):
     upper, x = divmod(place, 4)
@@ -333,26 +333,44 @@
     prompt_out = [
         remote(prb.at[seq], prb.at[seq], pr_s.at[d - 1], pr_r.at[seq], at_seq(d)) for d in (1, 3, 2)
     ]
+    pkv_up = remote(pkv.at[x], pkv.at[x], pk_s.at[3], pk_r.at[x], at_z)
     pkv_out = [remote(pkv.at[x], pkv.at[x], pk_s.at[d - 1], pk_r.at[x], at_x(d)) for d in (1, 3, 2)]
+
+    lower, upper = zh == 0, zh == 1
 
     def prompt_rows():
         loads[2].wait()
-        prb[seq] = normalized(prm[...].astype(F32)).astype(BF16)
+
+        @pl.when(lower)
+        def _():
+            prb[seq] = normalized(prm[...].astype(F32)).astype(BF16)
 
     def prompt_send():
-        for copy in prompt_out:
-            copy.start()
+        @pl.when(lower)
+        def _():
+            for copy in prompt_out:
+                copy.start()
 
     def prompt_project():
         loads[5].wait()
-        for d in (1, 3, 2):
-            c = (seq + d) % 4
-            remote(prb.at[c], prb.at[c], pr_s.at[0], pr_r.at[c], at_seq(1)).wait_recv()
-        rows = prb[...].reshape(64, model)
-        for j in range(2):
-            pkv[x, j] = jnp.dot(rows, wpr[j], preferred_element_type=F32).astype(BF16)
-        for copy in pkv_out:
-            copy.start()
+
+        @pl.when(lower)
+        def _():
+            for d in (1, 3, 2):
+                c = (seq + d) % 4
+                remote(prb.at[c], prb.at[c], pr_s.at[0], pr_r.at[c], at_seq(1)).wait_recv()
+            rows = prb[...].reshape(64, model)
+            for j in range(2):
+                pkv[x, j] = jnp.dot(rows, wpr[j], preferred_element_type=F32).astype(BF16)
+            for copy in [pkv_up] + pkv_out:
+                copy.start()
+
+    def prompt_pass():
+        @pl.when(upper)
+        def _():
+            pkv_up.wait_recv()
+            for copy in pkv_out:
+                copy.start()
 
     def prompt_attend():
         for d in (1, 3, 2):
@@ -451,11 +469,13 @@
         attend_next(index)
         if index == 1:
             prompt_project()
+        if index == 4:
+            prompt_pass()
         if index == 5:
             quarter_serve()
+            wout_serve()
+        if index == 6:
             prompt_attend()
-        if index == 6:
-            wout_serve()
 
     guide = guide_in[0]
     first_side = cfg == 0
@@ -488,8 +508,13 @@
         total = total + jnp.dot(mixall[c].reshape(128, width), wout[c], preferred_element_type=F32)
     out_ref[...] = (table[2, pl.ds(now, 1), half_cols] * total).astype(BF16)
 
-    for copy in sum(quarter_on, quarter_out) + mod_out[0] + mod_out[1] + prompt_out + pkv_out + wout_out + wout_pass + att_out + mix_out:
+    for copy in sum(quarter_on, quarter_out) + mod_out[0] + mod_out[1] + pkv_out + wout_out + wout_pass + att_out + mix_out:
         copy.wait_send()
+    @pl.when(lower)
+    def _():
+        for copy in [pkv_up] + prompt_out:
+            copy.wait_send()
+
     for direction in range(2):
         mod_forward(direction).wait_send()
     each_stale(early, lambda copy: copy.wait_send())
@@ -542,7 +567,7 @@
             pltpu.VMEM((4, 2, rows // 2, width), BF16),
             pltpu.VMEM((4, 2, rows // 2, width), BF16),
             dma((10,)), dma((3, 4)), dma((4, 4)), dma((2, 2)), dma((2, 2)), dma((2,)), dma((2,)),
-            dma((3,)), dma((4,)), dma((3,)), dma((4,)), dma((2,)), dma((2,)), dma((2,)), dma((2,)),
+            dma((3,)), dma((4,)), dma((4,)), dma((4,)), dma((2,)), dma((2,)), dma((2,)), dma((2,)),
             dma((18, 4)), dma((8, 4)), dma((3,)), dma((4,)), dma((3, 3)), dma((4, 4)), dma((heads,)), dma((heads,)), dma((heads, 3, 2)), dma((heads, 4, 2)),
         ],
         compiler_params=pltpu.CompilerParams(

time: 92 us -> 88.9 us (0.966)
  Pallas kernels: 88.8 us -> 85.6 us
    pallas_call x1, Pallas kernels: 88.8 us -> 85.6 us  [local(): pl.pallas_call(kernel, out_shape=jax.ShapeDtypeStruct((rows, half), BF16)...]
where the time goes in v6:
time: 88.9 us; the launch traced here: 88.7 us
  Pallas kernels  85.6 us (96%)
  local copies, waits for them, and re-layouts  1.77 us (2%)
  between operations  1.31 us (1%)
    pallas_call x1, Pallas kernels, local(): pl.pallas_call(kernel, out_shape=jax.ShapeDtypeStruct((rows, half), BF16)...  85.6 us

profile of v6, /device:TPU:6, one launch (start us, length us, event | category | flops | bytes accessed | tf_op | source)
XLA Modules:
  0.0 88.7 jit_solution(4231262348475825052)
XLA Ops:
  1.3 85.6 %guided_attention.1 = bf16[128,1536]{1,0:T(8,128)(2,1)} custom-call(bf16[1,128,3072]{2,1,0:T(8,128)(2,1)} %img_in.1, bf16[1,64,3072]{2,1,0:T(8,128)(2,1)} %prm_in.1, bf16[1,2,128,1536]{3,2,1,0:T(8,128)(2,1)} %stale_in.1, bf16[3,3072,384]{2,1,0:T(8,128)(2,1)} %wqkv_in.1, bf16[2,3072,384]{2,1,0:T(8,128)(2,1)} %wpr_in.1, bf16[384,3072]{1,0:T(8,128)(2,1)} %wout_in.1, ...), custom_call_target="tpu_custom_call" | custom-call | tf_op jit(solution)/shard_map/guided_attention/pallas_call | solution.py:545
  86.9 1.8 %copy.13 = bf16[128,1536]{1,0:T(8,128)(2,1)} copy(bf16[128,1536]{1,0:T(8,128)(2,1)} %guided_attention.1) | data formatting | bytes 786432

commit v7 on v6

--- a/solution.py
+++ b/solution.py
@@ -436,12 +436,12 @@
             wout_arrival(direction).wait_recv()
             wout_pass[direction].start()
 
-    def wout_last():
-        for direction in range(2):
-            wout_forward(direction, (seq + 2) % 4).wait_recv()
-        for d in (1, 3, 2):
-            for place in line_of:
-                quarter_arrival(d, place).wait_recv()
+    def wout_last(d):
+        if d == 2:
+            for direction in range(2):
+                wout_forward(direction, (seq + 2) % 4).wait_recv()
+        for place in line_of:
+            quarter_arrival(d, place).wait_recv()
 
     def mod_last():
         for direction in range(2):
@@ -498,8 +498,8 @@
             copy.start()
             mix_out.append(copy)
     total = jnp.dot(mix[0].reshape(128, width), wout[seq], preferred_element_type=F32)
-    wout_last()
     for d in (1, 3, 2):
+        wout_last(d)
         c = (seq + d) % 4
         for h in range(heads):
             for half in range(2):

time: 88.9 us -> 88.9 us (level)
  no operation moved by 1% of the time
where the time goes in v7:
time: 88.9 us; the launch traced here: 88.7 us
  Pallas kernels  85.6 us (96%)
  local copies, waits for them, and re-layouts  1.77 us (2%)
  between operations  1.31 us (1%)
    pallas_call x1, Pallas kernels, local(): pl.pallas_call(kernel, out_shape=jax.ShapeDtypeStruct((rows, half), BF16)...  85.6 us

profile of v7, /device:TPU:6, one launch (start us, length us, event | category | flops | bytes accessed | tf_op | source)
XLA Modules:
  0.0 88.7 jit_solution(6976783233304106093)
XLA Ops:
  1.3 85.6 %guided_attention.1 = bf16[128,1536]{1,0:T(8,128)(2,1)} custom-call(bf16[1,128,3072]{2,1,0:T(8,128)(2,1)} %img_in.1, bf16[1,64,3072]{2,1,0:T(8,128)(2,1)} %prm_in.1, bf16[1,2,128,1536]{3,2,1,0:T(8,128)(2,1)} %stale_in.1, bf16[3,3072,384]{2,1,0:T(8,128)(2,1)} %wqkv_in.1, bf16[2,3072,384]{2,1,0:T(8,128)(2,1)} %wpr_in.1, bf16[384,3072]{1,0:T(8,128)(2,1)} %wout_in.1, ...), custom_call_target="tpu_custom_call" | custom-call | tf_op jit(solution)/shard_map/guided_attention/pallas_call | solution.py:545
  86.9 1.8 %copy.13 = bf16[128,1536]{1,0:T(8,128)(2,1)} copy(bf16[128,1536]{1,0:T(8,128)(2,1)} %guided_attention.1) | data formatting | bytes 786432
